TPU v7x, 32 devices: a whole 2x2x4 slice. The times are simulated.
32 devices in a mesh: expert: 8 (over z, y), context: 2 (over core), dp: 2 (over x).
Axes of the slice: x: 2, y: 2, z: 4, core: 2. Of those that a mesh axis runs over, the one named last changes fastest.
Arguments:
- residual: bfloat16 [2, 2, 256, 4096], P('dp', 'context', 'expert'), may hold values from -6 to 6
- x_raw: bfloat16 [2, 2, 256, 8192], P('dp', 'context', None, 'expert'), may hold values from -6 to 6
- z_gate: bfloat16 [2, 2, 256, 8192], P('dp', 'context', None, 'expert'), may hold values from -6 to 6
- conv_w: float32 [4, 8192], P(None, 'expert'), may hold values from -3 to 3
- conv_b: float32 [8192], P('expert'), may hold values from -0.5 to 0.5
- xproj_w: bfloat16 [8192, 288], P('expert'), may hold values from -0.0625 to 0.0625
- dtproj_w: bfloat16 [256, 8192], P(None, 'expert'), may hold values from -0.375 to 0.375
- dt_bias: float32 [8192], P('expert'), may hold values from -4 to -1
- a_rate: float32 [16, 8192], P(None, 'expert'), may hold values from 0.02 to 2
- skip_gain: float32 [8192], P('expert'), may hold values from 0.5 to 1.5
- out_w: bfloat16 [8192, 4096], P('expert'), may hold values from -0.0625 to 0.0625
- norm_gain: float32 [4096], replicated, may hold values from 0.5 to 1.5
- route_ids: int32 [2, 2, 256, 2], P('dp', 'context', 'expert'), may hold values from 0 to 3, all different within a row; in each aligned block of 32 rows (0 to 31, 32 to 63, ..., all dimensions but the last counted through in order) at most 24 rows name the same one
- route_w: float32 [2, 2, 256, 2], P('dp', 'context', 'expert'), may hold values from 0.2 to 1
- w_gate: bfloat16 [8, 4096, 6144], P('expert', None, ('context', 'dp')), may hold values from -0.09375 to 0.09375
- w_up: bfloat16 [8, 4096, 6144], P('expert', None, ('context', 'dp')), may hold values from -0.09375 to 0.09375
- w_down: bfloat16 [8, 6144, 4096], P('expert', ('context', 'dp')), may hold values from -0.0546875 to 0.0546875
Outputs:
- mixed: bfloat16 [2, 2, 256, 4096], P('dp', 'context', 'expert')
Inputs may be any that keep to these rules, and one draw needn't show every extreme that they name: `route_ids`: each row names 2 different experts; in each aligned block of 32 rows no expert is named by more than 24 rows, a bound that some block reaches.
All inputs are finite; a program needn't handle non-finite values.
Results may differ from a plain program's by a relative error of at most 0.018.
Values may be sent and summed in bfloat16 or wider, within the bound.
No kernel may reach another device: no remote copies, remote signals or barrier semaphores. Data moves between devices by JAX's collectives and lax.ppermute only.
A program may use at most 192 MiB of HBM per device.

v0:
```python
import jax
import jax.numpy as jnp
from jax import lax
from jax.sharding import PartitionSpec as P

D = 4096
NSTATE = 16
DT_RANK = 256
CONV = 4
TOP = 2


def from_behind(block, axis, distance):
    devices = range(lax.axis_size(axis))
    route = [(i - distance, i) for i in devices if i - distance in devices]
    return lax.ppermute(block, axis, route)


def carried_in(x, axis, combine, identity):
    size, mine = (lax.axis_size(axis), lax.axis_index(axis))
    everything = jax.tree.map(
        lambda part, kind: lax.all_gather(part.astype(kind), axis), x, (jnp.bfloat16, jnp.bfloat16)
    )
    start = jax.tree.map(
        lambda part, zero: jnp.broadcast_to(jnp.asarray(zero, part.dtype), part.shape), x, identity
    )

    def turn(k, before):
        reached = k < mine
        new = combine(
            before, jax.tree.map(lambda part, own: part[k].astype(own.dtype), everything, x)
        )
        return jax.tree.map(lambda a, b: jnp.where(reached, a, b), new, before)

    return lax.fori_loop(0, size, turn, start)


def combine_pairs(earlier, later):
    return (earlier[0] * later[0], later[0] * earlier[1] + later[1])


def block_states(step_size, drives, a_rate, block_len):
    length = step_size.shape[0]
    count = length // block_len
    steps_blocked = step_size.reshape(count, block_len, step_size.shape[1])
    drives_blocked = drives.reshape(count, block_len, drives.shape[1], drives.shape[2])
    lower = jnp.arange(block_len)[:, None] >= jnp.arange(block_len)[None, :]

    def advance(carry, inputs):
        block_steps, block_drives = inputs
        local_cum = jnp.cumsum(block_steps, axis=0)
        spread = local_cum[:, None, :] - local_cum[None, :, :]
        spread = jnp.where(lower[:, :, None], spread, 0.0)
        weights = jnp.where(
            lower[:, :, None, None], jnp.exp(-spread[:, :, None, :] * a_rate[None, None, :, :]), 0.0
        )
        inside = jnp.sum(weights * block_drives[None, :, :, :], axis=1)
        carried = jnp.exp(-local_cum[:, None, :] * a_rate[None, :, :]) * carry[None]
        result = inside + carried
        return (result[-1], result)

    start = jnp.zeros((drives.shape[1], drives.shape[2]), jnp.float32)
    unused, blocked = lax.scan(advance, start, (steps_blocked, drives_blocked))
    return blocked.reshape(drives.shape)


def on_device(
    residual,
    x_raw,
    z_gate,
    conv_w,
    conv_b,
    xproj_w,
    dtproj_w,
    dt_bias,
    a_rate,
    skip_gain,
    out_w,
    norm_gain,
    route_ids,
    route_w,
    w_gate,
    w_up,
    w_down,
):
    length = x_raw.shape[2]
    values = x_raw[0, 0]
    prior_rim = from_behind(values[length - (CONV - 1) :], "context", 1)
    padded = jnp.concatenate([prior_rim, values], axis=0).astype(jnp.float32)
    conv_sum = conv_b[None, :] + sum(
        (
            conv_w[lag_index][None, :] * padded[lag_index : lag_index + length]
            for lag_index in range(CONV)
        )
    )
    mixed_in = jax.nn.silu(conv_sum).astype(jnp.bfloat16)
    projected = lax.psum(
        jnp.dot(mixed_in, xproj_w, preferred_element_type=jnp.float32).astype(jnp.bfloat16),
        "expert",
    ).astype(jnp.float32)
    dt_low = projected[:, :DT_RANK].astype(jnp.bfloat16)
    b_in = projected[:, DT_RANK : DT_RANK + NSTATE]
    c_out = projected[:, DT_RANK + NSTATE :]
    step_size = jax.nn.softplus(
        jnp.dot(dt_low, dtproj_w, preferred_element_type=jnp.float32) + dt_bias[None, :]
    )
    inner_in = mixed_in.astype(jnp.float32)
    drives = (step_size * inner_in)[:, None, :] * b_in[:, :, None]
    states = block_states(step_size, drives, a_rate, 16)
    total_steps = jnp.cumsum(step_size, axis=0)
    cumulated = jnp.exp(-total_steps[:, None, :] * a_rate[None, :, :])
    identity = (jnp.ones_like(cumulated[-1]), jnp.zeros_like(states[-1]))
    entering = carried_in((cumulated[-1], states[-1]), "context", combine_pairs, identity)
    states = states + cumulated * entering[1][None]
    readout = jnp.sum(c_out[:, :, None] * states, axis=1) + skip_gain[None, :] * inner_in
    gated = (readout * jax.nn.silu(z_gate[0, 0].astype(jnp.float32))).astype(jnp.bfloat16)
    partial_out = jnp.dot(gated, out_w, preferred_element_type=jnp.float32)
    row_count = residual.shape[2]
    mixer_out = lax.psum_scatter(
        partial_out.astype(jnp.bfloat16), "expert", scatter_dimension=0, tiled=True
    ).astype(jnp.float32)
    stream_f = (
        (residual[0, 0].astype(jnp.float32) + mixer_out).astype(jnp.bfloat16).astype(jnp.float32)
    )
    normed = (
        stream_f
        * lax.rsqrt(jnp.mean(stream_f * stream_f, axis=1, keepdims=True) + 1e-05)
        * norm_gain[None, :]
    ).astype(jnp.bfloat16)
    choices_flat = route_ids[0, 0].reshape(-1)
    weights_flat = route_w[0, 0].reshape(-1)
    experts = lax.axis_size("expert") // 2
    capacity = min(row_count, 8 * ((3 * row_count * TOP + 16 * experts - 1) // (16 * experts)))
    onehot = (choices_flat[:, None] == jnp.arange(experts, dtype=jnp.int32)[None, :]).astype(
        jnp.int32
    )
    ranking = jnp.sum(onehot * (jnp.cumsum(onehot, axis=0) - 1), axis=1)
    slot_of = choices_flat * capacity + ranking
    placing = (jnp.arange(experts * capacity, dtype=jnp.int32)[:, None] == slot_of[None, :]).astype(
        jnp.bfloat16
    )
    sources = jnp.repeat(normed, TOP, axis=0)
    packed = jnp.dot(placing, sources, preferred_element_type=jnp.float32).astype(jnp.bfloat16)
    packed = packed.reshape(experts, 1, capacity, D)
    outgoing = jnp.broadcast_to(packed, (experts, 2, capacity, D)).reshape(2 * experts, capacity, D)
    incoming = lax.all_to_all(outgoing, "expert", split_axis=0, concat_axis=0, tiled=True)
    flat_rows = incoming.reshape(2 * experts * capacity, D)
    gate_local = w_gate[0]
    up_local = w_up[0]
    down_local = w_down[0]
    block_rows = lax.all_gather(flat_rows, ("context", "dp"), axis=0, tiled=True)
    gate_val = jnp.dot(block_rows, gate_local, preferred_element_type=jnp.float32)
    up_val = jnp.dot(block_rows, up_local, preferred_element_type=jnp.float32)
    hidden = (jax.nn.silu(gate_val) * up_val).astype(jnp.bfloat16)
    partials = jnp.dot(hidden, down_local, preferred_element_type=jnp.float32)
    own_share = lax.psum_scatter(
        partials.astype(jnp.bfloat16), ("context", "dp"), scatter_dimension=0, tiled=True
    )
    outbound = own_share.reshape(2 * experts, capacity, D)
    came_back = lax.all_to_all(outbound, "expert", split_axis=0, concat_axis=0, tiled=True)
    both_halves = jnp.sum(came_back.astype(jnp.float32).reshape(experts, 2, capacity, D), axis=1)
    both_halves = both_halves.reshape(experts * capacity, D)
    picked = jnp.take(both_halves, slot_of, axis=0)
    expert_sum = jnp.sum((picked * weights_flat[:, None]).reshape(row_count, TOP, D), axis=1)
    mixed = (stream_f + expert_sum).astype(jnp.bfloat16)
    return mixed.reshape(1, 1, row_count, D)


def solution(mesh):
    placed = (
        P("dp", "context", "expert", None),
        P("dp", "context", None, "expert"),
        P("dp", "context", None, "expert"),
        P(None, "expert"),
        P("expert"),
        P("expert", None),
        P(None, "expert"),
        P("expert"),
        P(None, "expert"),
        P("expert"),
        P("expert", None),
        P(),
        P("dp", "context", "expert", None),
        P("dp", "context", "expert", None),
        P("expert", None, ("context", "dp")),
        P("expert", None, ("context", "dp")),
        P("expert", ("context", "dp"), None),
    )
    return jax.shard_map(
        on_device,
        mesh=mesh,
        in_specs=placed,
        out_specs=P("dp", "context", "expert", None),
        check_vma=False,
    )
```

profile of v0, /device:TPU:0, one launch (start us, length us, event | category | flops | bytes accessed | tf_op | source)
XLA Modules:
  0.0 575.3 jit_solution(17556054295870510677)
XLA Ops:
  7.3 2.3 collective-permute-start
  14.3 72.0 %all-reduce.2.cloned.1.call-done = bf16[256,288]{0,1:T(8,128)(2,1)} async-done(((bf16[256,288]{0,1:T(8,128)(2,1)}), bf16[256,288]{0,1:T(8,128)(2,1)}) %all-reduce.2.cloned.1.call-update) | async-done | bytes 147472 | tf_op jit(solution)/shard_map/psum | solution.py:97
  87.1 2.9 convert_multiply_fusion.3
  90.0 7.0 %broadcast_multiply_fusion = f32[16,16,16,1024]{3,2,1,0:T(8,128)} fusion(f32[16,16,16]{2,1,0:T(8,128)S(1)} %bitcast.143, f32[16,16,1024]{2,1,0:T(8,128)S(1)} %bitcast.136), kind=kLoop, calls=%fused_computation.21 | loop fusion | flops 4194304 | bytes 17842176 | tf_op jit(solution)/shard_map/mul | solution.py:108
  97.0 129.9 %while.28 = (s32[]{:T(128)}, f32[16,1024]{1,0:T(8,128)S(1)}, f32[16,16,16,1024]{3,2,1,0:T(8,128)}, f32[16,16,1024]{2,1,0:T(8,128)}, f32[16,1024]{1,0:T(8,128)S(1...) while((s32[]{:T(128)}, f32[16,1024]{1,0:T(8,128)S(1)}, ...), condition=%wide.region_4.5_spmd.clone.clone, body=%wide.region_1.4_spmd.clone.clone.sunk | while | flops 18399488 | bytes 9516385 | solution.py:63
  99.4 4.4 multiply_reduce_fusion.4
  107.5 4.4 multiply_reduce_fusion.4
  115.7 4.4 multiply_reduce_fusion.4
  123.8 4.4 multiply_reduce_fusion.4
  131.9 4.4 multiply_reduce_fusion.4
  140.0 4.4 multiply_reduce_fusion.4
  148.1 4.4 multiply_reduce_fusion.4
  156.3 4.4 multiply_reduce_fusion.4
  164.4 4.4 multiply_reduce_fusion.4
  172.6 4.4 multiply_reduce_fusion.4
  180.6 4.4 multiply_reduce_fusion.4
  188.7 4.4 multiply_reduce_fusion.4
  196.8 4.4 multiply_reduce_fusion.4
  205.0 4.4 multiply_reduce_fusion.4
  213.1 4.4 multiply_reduce_fusion.4
  221.2 4.4 multiply_reduce_fusion.4
  226.9 6.6 %convert.14 = bf16[16,16,16,1024]{3,2,1,0:T(8,128)(2,1)S(1)} convert(f32[16,16,16,1024]{3,2,1,0:T(8,128)} %get-tuple-element.139) | non-fusion elementwise | flops 4194304 | bytes 25165824 | tf_op jit(solution)/shard_map/convert.6
  239.5 9.4 %multiply_reduce_fusion.1 = f32[16,16,1024]{2,1,0:T(8,128)S(1)} fusion(f32[16,16,16,1024]{3,2,1,0:T(8,128)} %get-tuple-element.139, f32[16,1024]{1,0:T(8,128)S(1)} %get-tuple-element.140, f32[16,1024]{1,0:T(8,128)S(1)} %get-tuple-element.339, f32[16,16,1024]{2,1,0:T(8,128)S(1)} %bitcast.135, f32[16,16,16]{2,1,0:T(8,128)S(1)} %bitcast.144), kind=kLoop, calls=%fused_computation.14 | loop fusion | flops 20709376 | bytes 19021824 | tf_op jit(solution)/shard_map/reduce_sum | solution.py:115
  249.9 7.1 %convolution_convert_fusion = bf16[256,4096]{1,0:T(8,128)(2,1)} fusion(bf16[256,1024]{1,0:T(8,128)(2,1)S(1)} %fusion.20, bf16[1024,4096]{1,0:T(8,128)(2,1)} %param.31), kind=kOutput, calls=%fused_computation.23 | convolution fusion | flops 2148532224 | bytes 11010048 | tf_op jit(solution)/shard_map/dot_general | solution.py:117
  257.7 66.9 %reduce-scatter.3.cloned.1.call-done = bf16[32,4096]{1,0:T(8,128)(2,1)} async-done(((bf16[256,4096]{1,0:T(8,128)(2,1)}), bf16[32,4096]{1,0:T(8,128)(2,1)}) %reduce-scatter.3.cloned.1.call-update) | async-done | bytes 262160 | tf_op jit(solution)/shard_map/reduce_scatter | solution.py:119
  328.1 39.3 %all_to_all.10 = bf16[8,24,4096]{2,1,0:T(8,128)(2,1)} all-to-all(bf16[8,24,4096]{2,1,0:T(8,128)(2,1)S(1)} %bitcast.132), channel_id=1, replica_groups=mesh['expert'=8,'context'=2,'dp'=2] {'expert'}, dimensions={0} | all-to-all | bytes 3145728 | tf_op jit(solution)/shard_map/all_to_all | solution.py:146
  367.7 45.2 %all-gather.2.cloned.1.call-done = bf16[768,4096]{1,0:T(8,128)(2,1)} async-done(((bf16[192,4096]{1,0:T(8,128)(2,1)}), bf16[768,4096]{1,0:T(8,128)(2,1)}) %all-gather.2.cloned.1.call-update) | async-done | bytes 6291472 | tf_op jit(solution)/shard_map/all_gather | solution.py:151
  413.0 16.1 %fusion.7 = f32[768,1536]{1,0:T(8,128)} fusion(bf16[768,4096]{1,0:T(8,128)(2,1)} %all-gather.2.cloned.1.call-done, bf16[1,4096,1536]{2,1,0:T(8,128)(2,1)} %param.36), kind=kOutput, calls=%fused_computation.17 | convolution fusion | flops 9663676416 | bytes 23592960 | tf_op jit(solution)/shard_map/dot_general | solution.py:153
  429.1 31.7 %fusion.11 = bf16[768,4096]{1,0:T(8,128)(2,1)} fusion(bf16[1,1536,4096]{2,1,0:T(8,128)(2,1)} %param.37, f32[768,1536]{1,0:T(8,128)} %fusion.7, bf16[768,4096]{1,0:T(8,128)(2,1)} %all-gather.2.cloned.1.call-done, bf16[1,4096,1536]{2,1,0:T(8,128)(2,1)} %param.35), kind=kOutput, calls=%fused_computation.22 | convolution fusion | flops 19337576448 | bytes 42467328 | tf_op jit(solution)/shard_map/dot_general | solution.py:155
  460.8 58.5 %reduce-scatter.5.cloned.1.call-done = bf16[192,4096]{1,0:T(8,128)(2,1)} async-done(((bf16[768,4096]{1,0:T(8,128)(2,1)}), bf16[192,4096]{1,0:T(8,128)(2,1)}) %reduce-scatter.5.cloned.1.call-update) | async-done | bytes 1572880 | tf_op jit(solution)/shard_map/reduce_scatter | solution.py:156
  519.3 5.5 all-to-all-start.1
  525.5 36.5 %all-to-all-done.1 = bf16[8,24,4096]{2,1,0:T(8,128)(2,1)} async-done(((bf16[8,24,4096]{2,1,0:T(8,128)(2,1)}), bf16[8,24,4096]{2,1,0:T(8,128)(2,1)}, u32[]{:S(2)}, u32[]{:S(2)}) %all-to-all-start.1) | async-done | bytes 1572896 | tf_op jit(solution)/shard_map/all_to_all | solution.py:160
  (253 shorter events, 83.3 us)
Async XLA Ops:
  6.5 6.6 %copy-start = (bf16[1024,288]{0,1:T(8,128)(2,1)S(1)}, bf16[1024,288]{0,1:T(8,128)(2,1)}, u32[]{:S(2)}) copy-start(bf16[1024,288]{0,1:T(8,128)(2,1)} %param.26) | copy-start | bytes 1769476
  6.5 79.7 %all-reduce.2.cloned.1.call-start = ((), (), s32[]{:S(2)}) async-start(), calls=%async_computation.4 | async-start | bytes 294912 | tf_op jit(solution)/shard_map/psum | solution.py:97
  7.3 3.2 collective-permute-start
  14.2 310.4 %reduce-scatter.3.cloned.1.call-start = ((), (), s32[]{:S(2)}) async-start(), calls=%async_computation.5 | async-start | bytes 2359296 | tf_op jit(solution)/shard_map/reduce_scatter | solution.py:119
  90.0 7.0 %copy-start.2 = (f32[16,1024]{1,0:T(8,128)S(1)}, f32[16,1024]{1,0:T(8,128)}, u32[]{:S(2)}) copy-start(f32[16,1024]{1,0:T(8,128)} %param.29) | copy-start | bytes 196612
  239.5 9.4 %copy-start.5 = (bf16[1,1,256,1024]{3,2,1,0:T(8,128)(2,1)S(1)}, bf16[1,1,256,1024]{3,2,1,0:T(8,128)(2,1)}, u32[]{:S(2)}) copy-start(bf16[1,1,256,1024]{3,2,1,0:T(8,128)(2,1)} %param.23) | copy-start | bytes 1572868
  239.5 9.4 %copy-start.7 = (f32[1024]{0:T(1024)S(1)}, f32[1024]{0:T(1024)}, u32[]{:S(2)}) copy-start(f32[1024]{0:T(1024)} %param.25) | copy-start | bytes 12292
  239.5 9.4 %copy-start.10 = (f32[1024]{0:T(1024)S(1)}, f32[1024]{0:T(1024)}, u32[]{:S(2)}) copy-start(f32[1024]{0:T(1024)} %param.30) | copy-start | bytes 12292
  249.9 7.2 %copy-start.8 = (s32[1,1,32,2]{2,3,1,0:T(2,128)S(1)}, s32[1,1,32,2]{2,3,1,0:T(2,128)}, u32[]{:S(2)}) copy-start(s32[1,1,32,2]{2,3,1,0:T(2,128)} %param.33) | copy-start | bytes 772
  249.9 74.7 %copy-start.3 = (bf16[1,1,32,4096]{3,2,1,0:T(8,128)(2,1)S(1)}, bf16[1,1,32,4096]{3,2,1,0:T(8,128)(2,1)}, u32[]{:S(2)}) copy-start(bf16[1,1,32,4096]{3,2,1,0:T(8,128)(2,1)} %param.21) | copy-start | bytes 786436
  249.9 75.9 %copy-start.6 = (f32[4096]{0:T(1024)S(1)}, f32[4096]{0:T(1024)}, u32[]{:S(2)}) copy-start(f32[4096]{0:T(1024)} %param.32) | copy-start | bytes 49156
  257.1 155.9 %all-gather.2.cloned.1.call-start = ((), (), s32[]{:S(2)}) async-start(), calls=%async_computation.6 | async-start | bytes 7864320 | tf_op jit(solution)/shard_map/all_gather | solution.py:151
  257.7 171.4 %copy-start.11 = (s32[64]{0:T(128)}, s32[64]{0:T(128)S(1)}, u32[]{:S(2)}) copy-start(s32[64]{0:T(128)S(1)} %select_reduce_fusion) | copy-start | bytes 772
  367.4 151.9 %reduce-scatter.5.cloned.1.call-start = ((), (), s32[]{:S(2)}) async-start(), calls=%async_computation.7 | async-start | bytes 7864320 | tf_op jit(solution)/shard_map/reduce_scatter | solution.py:156
  460.7 64.1 %copy-start.12 = (s32[64]{0:T(128)S(1)}, s32[64]{0:T(128)}, u32[]{:S(2)}) copy-start(s32[64]{0:T(128)} %copy-done.11) | copy-start | bytes 772
  460.7 64.2 %copy-start.9 = (s32[1,1,32,2]{2,3,1,0:T(2,128)S(1)}, s32[1,1,32,2]{2,3,1,0:T(2,128)}, u32[]{:S(2)}) copy-start(s32[1,1,32,2]{2,3,1,0:T(2,128)} %param.33) | copy-start | bytes 772
  460.7 64.6 %copy-start.13 = (f32[1,1,32,2]{2,3,1,0:T(2,128)S(1)}, f32[1,1,32,2]{2,3,1,0:T(2,128)}, u32[]{:S(2)}) copy-start(f32[1,1,32,2]{2,3,1,0:T(2,128)} %param.34) | copy-start | bytes 772
  519.3 42.6 %all-to-all-start.1 = ((bf16[8,24,4096]{2,1,0:T(8,128)(2,1)}), bf16[8,24,4096]{2,1,0:T(8,128)(2,1)}, u32[]{:S(2)}, u32[]{:S(2)}) async-start(bf16[8,24,4096]{2,1,0:T(8,128)(2,1)} %bitcast.141), calls=%async_computation.3 | async-start | bytes 3145728 | tf_op jit(solution)/shard_map/all_to_all | solution.py:160
  524.8 42.2 %copy-start.4 = (bf16[1,1,32,4096]{3,2,1,0:T(8,128)(2,1)S(1)}, bf16[1,1,32,4096]{3,2,1,0:T(8,128)(2,1)}, u32[]{:S(2)}) copy-start(bf16[1,1,32,4096]{3,2,1,0:T(8,128)(2,1)} %param.21) | copy-start | bytes 786436
  525.4 43.3 %copy-start.1 = (bf16[1024,288]{0,1:T(8,128)(2,1)S(1)}, bf16[1024,288]{0,1:T(8,128)(2,1)}, u32[]{:S(2)}) copy-start(bf16[1024,288]{0,1:T(8,128)(2,1)} %param.26) | copy-start | bytes 1769476
Sparse Core Ops, SparseCore 0:
  14.3 71.8 all-reduce.1
  257.2 67.3 reduce-scatter.2
  367.6 45.3 all-gather.1
  460.9 58.3 reduce-scatter.4
where the time goes:
time: 577 us; the launch traced here: 575 us
  waiting for transfers between devices  279 us (48%)
  other arithmetic  130 us (23%)
  matrix products  59.1 us (10%)
  blocking collectives  43.2 us (7%)
  local copies, waits for them, and re-layouts  40.7 us (7%)
  between operations  13.5 us (2%)
  starting transfers between devices  8.21 us (1%)
    psum x1, waiting for transfers between devices, on_device(): lax.psum(jnp.dot(mixed_in, xproj_w, preferred_element_type=jnp.float32).a...  72 us
    reduce_sum x16, other arithmetic, advance(): inside = jnp.sum(weights * block_drives[None, :, :, :], axis=1)  70.5 us
    reduce_scatter x1, waiting for transfers between devices, on_device(): lax.psum_scatter(partial_out.astype(jnp.bfloat16), 'expert', scatter_dime...  66.9 us
    reduce_scatter x1, waiting for transfers between devices, on_device(): lax.psum_scatter(partials.astype(jnp.bfloat16), ('context', 'dp'), scatte...  58.5 us
    all_gather x1, waiting for transfers between devices, on_device(): lax.all_gather(flat_rows, ('context', 'dp'), axis=0, tiled=True)  45.2 us
    all_to_all x1, blocking collectives, on_device(): lax.all_to_all(outgoing, 'expert', split_axis=0, concat_axis=0, tiled=True)  39.3 us
    all_to_all x1, waiting for transfers between devices, on_device(): lax.all_to_all(outbound, 'expert', split_axis=0, concat_axis=0, tiled=True)  36.5 us
    dot_general x1, matrix products, on_device(): partials = jnp.dot(hidden, down_local, preferred_element_type=jnp.float32)  31.7 us
  transfers between devices with their start and end apart: 6, of which 5 were waited for; matrix products, arithmetic and copies ran while one was open for 0% of the time, Pallas kernels for 0%

commit v1 on v0

v1 whole, which is shorter than its diff:
```python
import functools

import jax
import jax.numpy as jnp
from jax import lax
from jax.experimental import pallas as pl
from jax.experimental.pallas import tpu as pltpu
from jax.sharding import PartitionSpec as P

NSTATE = 16
DT_RANK = 256
CONV = 4
TOP = 2
LANES = 128
SUB = 8
F32 = jnp.float32
BF16 = jnp.bfloat16
MIB = 1 << 20


def from_behind(block, axis, distance):
    devices = range(lax.axis_size(axis))
    route = [(i - distance, i) for i in devices if i - distance in devices]
    return lax.ppermute(block, axis, route)


def shift(block, axis, distance):
    size = lax.axis_size(axis)
    return lax.ppermute(block, axis, [(i, (i + distance) % size) for i in range(size)])


def swap_pair(block):
    size = lax.axis_size("expert")
    return lax.ppermute(block, "expert", [(i, i ^ 1) for i in range(size)])


def cost(flops, bytes_accessed, transcendentals=0):
    return pl.CostEstimate(
        flops=int(flops), bytes_accessed=int(bytes_accessed), transcendentals=int(transcendentals)
    )


def spread_rows(values, wide_ref):
    length, count = values.shape
    col = lax.broadcasted_iota(jnp.int32, (count, count * LANES), 1)
    row = lax.broadcasted_iota(jnp.int32, (count, count * LANES), 0)
    ones = jnp.where((col >= row * LANES) & (col < (row + 1) * LANES), 1.0, 0.0).astype(BF16)
    out = jnp.dot(values, ones, preferred_element_type=F32)
    for n in range(count):
        wide_ref[pl.ds(n * length, length), :] = out[:, n * LANES : (n + 1) * LANES]


def scan_kernel(groups, low_ref, bc_ref, w_ref, bias_ref, neg_ref, x_ref, y_ref, sum_ref, end_ref,
                step_ref, drive_ref, wide_ref):
    length = x_ref.shape[0]
    spread_rows(bc_ref[...], wide_ref)
    for g in range(SUB):
        rows = pl.ds(g, length, stride=SUB)
        if g >= groups:
            step_ref[rows, :] = jnp.zeros((length, LANES), F32)
            drive_ref[rows, :] = jnp.zeros((length, LANES), F32)
            continue
        cols = pl.ds(g * LANES, LANES)
        raw = jnp.dot(low_ref[...], w_ref[:, cols], preferred_element_type=F32) + bias_ref[:, cols]
        step = jnp.maximum(raw, 0.0) + jnp.log1p(jnp.exp(-jnp.abs(raw)))
        step_ref[rows, :] = step
        drive_ref[rows, :] = step * x_ref[:, cols].astype(F32)

    def block(k, carry):
        states, total = list(carry[0]), carry[1]
        for u in range(SUB):
            t = k * SUB + u
            here = pl.ds(pl.multiple_of(t * SUB, SUB), SUB)
            step, drive = step_ref[here, :], drive_ref[here, :]
            total = total + step
            out = jnp.zeros((SUB, LANES), F32)
            for n in range(NSTATE):
                decay = jnp.exp(step * neg_ref[n])
                b = wide_ref[pl.ds(n * length + t, 1), :]
                c = wide_ref[pl.ds((NSTATE + n) * length + t, 1), :]
                states[n] = states[n] * decay + drive * b
                out = out + states[n] * c
            y_ref[here, :] = out
            sum_ref[here, :] = total
        return tuple(states), total

    zero = jnp.zeros((SUB, LANES), F32)
    states, total = lax.fori_loop(0, length // SUB, block, ((zero,) * NSTATE, zero))
    for n in range(NSTATE):
        end_ref[n] = states[n]


def run_scan(low, bc, w, bias, neg, x):
    length, channels = x.shape
    vmem = pl.BlockSpec(memory_space=pltpu.VMEM)
    tall = jax.ShapeDtypeStruct((length * SUB, LANES), F32)
    return pl.pallas_call(
        functools.partial(scan_kernel, channels // LANES),
        out_shape=(tall, tall, jax.ShapeDtypeStruct((NSTATE, SUB, LANES), F32)),
        in_specs=[vmem] * 6,
        out_specs=(vmem,) * 3,
        scratch_shapes=[
            pltpu.VMEM((length * SUB, LANES), F32),
            pltpu.VMEM((length * SUB, LANES), F32),
            pltpu.VMEM((2 * NSTATE * length, LANES), F32),
        ],
        compiler_params=pltpu.CompilerParams(vmem_limit_bytes=24 * MIB),
        cost_estimate=cost(2e8, 4 * MIB, NSTATE * length * channels),
        name="state_scan",
    )(low, bc, w, bias, neg, x)


def out_kernel(groups, piece, half_ref, y_ref, sum_ref, enter_ref, c_ref, neg_ref, x_ref, z_ref,
               skip_ref, w_hbm, kept_ref, sent_ref, full_ref, wide_ref, gated_ref, order_ref, w_ref,
               sem):
    length = x_ref.shape[0]
    fetch = pltpu.make_async_copy(w_hbm, w_ref, sem)
    fetch.start()
    spread_rows(c_ref[...], wide_ref)

    def block(k, carry):
        for u in range(SUB):
            t = k * SUB + u
            here = pl.ds(pl.multiple_of(t * SUB, SUB), SUB)
            total = sum_ref[here, :]
            out = y_ref[here, :]
            for n in range(NSTATE):
                c = wide_ref[pl.ds(n * length + t, 1), :]
                out = out + jnp.exp(total * neg_ref[n]) * enter_ref[n] * c
            full_ref[here, :] = out
        return carry

    lax.fori_loop(0, length // SUB, block, 0)
    for g in range(groups):
        cols = pl.ds(g * LANES, LANES)
        mixed_in = x_ref[:, cols].astype(F32)
        read = full_ref[pl.ds(g, length, stride=SUB), :] + skip_ref[:, cols] * mixed_in
        z = z_ref[:, cols].astype(F32)
        gated_ref[:, cols] = (read * (z / (1.0 + jnp.exp(-z)))).astype(BF16)
    half = half_ref[0]
    count = length // 2
    for k in range(count // piece):
        for r in range(2):
            source = pl.multiple_of((2 * k + (half ^ r)) * piece, piece)
            order_ref[pl.ds(r * count + k * piece, piece), :] = gated_ref[pl.ds(source, piece), :]
    fetch.wait()
    wide = w_ref.shape[1]
    tile = min(512, wide)
    for j in range(wide // tile):
        cols = pl.ds(j * tile, tile)
        out = jnp.dot(order_ref[...], w_ref[:, cols], preferred_element_type=F32).astype(BF16)
        kept_ref[:, cols] = out[:count]
        sent_ref[:, cols] = out[count:]


def run_out(half, piece, y, total, enter, c, neg, x, z, skip, w):
    length, channels = x.shape
    wide = w.shape[1]
    vmem = pl.BlockSpec(memory_space=pltpu.VMEM)
    part = jax.ShapeDtypeStruct((length // 2, wide), BF16)
    return pl.pallas_call(
        functools.partial(out_kernel, channels // LANES, piece),
        out_shape=(part, part),
        in_specs=[pl.BlockSpec(memory_space=pltpu.SMEM)] + [vmem] * 8 + [pl.BlockSpec(memory_space=pl.ANY)],
        out_specs=(vmem, vmem),
        scratch_shapes=[
            pltpu.VMEM((length * SUB, LANES), F32),
            pltpu.VMEM((NSTATE * length, LANES), F32),
            pltpu.VMEM((length, channels), BF16),
            pltpu.VMEM((length, channels), BF16),
            pltpu.VMEM((channels, wide), BF16),
            pltpu.SemaphoreType.DMA,
        ],
        compiler_params=pltpu.CompilerParams(vmem_limit_bytes=32 * MIB),
        cost_estimate=cost(
            2 * length * channels * wide, 2 * channels * wide + 8 * MIB, NSTATE * length * channels
        ),
        name="readout_project",
    )(half, y, total, enter, c, neg, x, z, skip, w)


def gate_up_kernel(count, *refs):
    pieces, (gate_ref, up_ref, out_ref, rows_ref) = refs[:count], refs[count:]

    @pl.when(pl.program_id(0) == 0)
    def _():
        at = 0
        for piece in pieces:
            rows_ref[pl.ds(at, piece.shape[0]), :] = piece[...]
            at += piece.shape[0]

    gate = jnp.dot(rows_ref[...], gate_ref[...], preferred_element_type=F32)
    up = jnp.dot(rows_ref[...], up_ref[...], preferred_element_type=F32)
    out_ref[...] = (gate / (1.0 + jnp.exp(-gate)) * up).astype(BF16)


def gate_up(pieces, w_gate, w_up):
    depth, hidden = w_gate.shape
    rows = sum(p.shape[0] for p in pieces)
    tile = min(256, hidden)
    fixed = [pl.BlockSpec(p.shape, lambda j: (0, 0)) for p in pieces]
    weight = pl.BlockSpec((depth, tile), lambda j: (0, j))
    return pl.pallas_call(
        functools.partial(gate_up_kernel, len(pieces)),
        out_shape=jax.ShapeDtypeStruct((rows, hidden), BF16),
        grid=(hidden // tile,),
        in_specs=fixed + [weight, weight],
        out_specs=pl.BlockSpec((rows, tile), lambda j: (0, j)),
        scratch_shapes=[pltpu.VMEM((rows, depth), BF16)],
        compiler_params=pltpu.CompilerParams(vmem_limit_bytes=40 * MIB),
        cost_estimate=cost(4 * rows * depth * hidden, 4 * depth * hidden + 2 * rows * depth),
        name="gate_up",
    )(*pieces, w_gate, w_up)


def down_kernel(count, places, *refs):
    pieces, (w_ref, own_ref, far_ref, rows_ref) = refs[:count], refs[count:]

    @pl.when(pl.program_id(0) == 0)
    def _():
        for source, start, target, size in places:
            rows_ref[pl.ds(target, size), :] = pieces[source][pl.ds(start, size), :]

    near = own_ref.shape[0]
    out = jnp.dot(rows_ref[...], w_ref[...], preferred_element_type=F32).astype(BF16)
    own_ref[...] = out[:near]
    far_ref[...] = out[near:]


def down(pieces, places, near, w_down, first, width):
    hidden = w_down.shape[0]
    rows = sum(p.shape[0] for p in pieces)
    tile = min(512, width)
    offset = first // tile
    fixed = [pl.BlockSpec(p.shape, lambda j: (0, 0)) for p in pieces]
    return pl.pallas_call(
        functools.partial(down_kernel, len(pieces), places),
        out_shape=(
            jax.ShapeDtypeStruct((near, width), BF16),
            jax.ShapeDtypeStruct((rows - near, width), BF16),
        ),
        grid=(width // tile,),
        in_specs=fixed + [pl.BlockSpec((hidden, tile), lambda j: (0, j + offset))],
        out_specs=(
            pl.BlockSpec((near, tile), lambda j: (0, j)),
            pl.BlockSpec((rows - near, tile), lambda j: (0, j)),
        ),
        scratch_shapes=[pltpu.VMEM((rows, hidden), BF16)],
        compiler_params=pltpu.CompilerParams(vmem_limit_bytes=32 * MIB),
        cost_estimate=cost(2 * rows * hidden * width, 2 * hidden * width + 2 * rows * (hidden + width)),
        name="down",
    )(*pieces, w_down)


def add_up(*parts):
    return sum(p.astype(F32) for p in parts)


def line_sum(blocks, place):
    size = blocks.shape[0]
    forth, back = [], []
    for s in range(1, size):
        forth.append([(2 * i + o, 2 * i + o + 2) for i in range(s) for o in range(2)])
        back.append([(2 * i + o, 2 * i + o - 2) for i in range(size - s, size) for o in range(2)])

    def block(k):
        return lax.dynamic_index_in_dim(blocks, jnp.clip(k, 0, size - 1), 0, keepdims=False)

    up, low = block(place + size - 1), block(place - size + 1)
    for s in range(1, size):
        up = lax.ppermute(up.astype(BF16), "expert", forth[s - 1]).astype(F32)
        low = lax.ppermute(low.astype(BF16), "expert", back[s - 1]).astype(F32)
        if s < size - 1:
            up = up + block(place + size - 1 - s)
            low = low + block(place - size + 1 + s)
    return block(place) + up + low


def on_device(
    residual,
    x_raw,
    z_gate,
    conv_w,
    conv_b,
    xproj_w,
    dtproj_w,
    dt_bias,
    a_rate,
    skip_gain,
    out_w,
    norm_gain,
    route_ids,
    route_w,
    w_gate,
    w_up,
    w_down,
):
    owners, contexts, dps = (lax.axis_size(a) for a in ("expert", "context", "dp"))
    me = lax.axis_index("expert")
    place, half = me // 2, me % 2
    line = owners // 2
    length, channels = x_raw.shape[2:]
    width = residual.shape[3]
    row_count = residual.shape[2]

    values = x_raw[0, 0]
    prior_rim = from_behind(values[length - (CONV - 1) :], "context", 1)
    padded = jnp.concatenate([prior_rim, values], axis=0).astype(F32)
    conv_sum = conv_b[None, :] + sum(
        (
            conv_w[lag_index][None, :] * padded[lag_index : lag_index + length]
            for lag_index in range(CONV)
        )
    )
    mixed_in = jax.nn.silu(conv_sum).astype(BF16)
    projected = jnp.dot(mixed_in, xproj_w, preferred_element_type=F32).astype(BF16)
    shares = lax.all_to_all(
        projected.reshape(owners, length // owners, -1), "expert", split_axis=0, concat_axis=0, tiled=True
    )
    share = add_up(*[shares[i] for i in range(owners)]).astype(BF16)
    projected = lax.all_to_all(
        jnp.broadcast_to(share[None], (owners,) + share.shape),
        "expert",
        split_axis=0,
        concat_axis=0,
        tiled=True,
    ).reshape(length, -1)
    dt_low = projected[:, :DT_RANK]
    bc = projected[:, DT_RANK:]

    neg = -a_rate.reshape(NSTATE, channels // LANES, LANES)
    neg = jnp.pad(neg, ((0, 0), (0, SUB - channels // LANES), (0, 0)))
    y, total, end = run_scan(dt_low, bc, dtproj_w, dt_bias[None, :], neg, mixed_in)
    enter = from_behind(end, "context", 1)
    for step in range(contexts - 2):
        decay = jnp.exp(total[-SUB:][None] * neg)
        enter = from_behind(end + decay * enter, "context", 1)
    kept, sent = run_out(
        half.astype(jnp.int32).reshape(1),
        row_count,
        y,
        total,
        enter,
        bc[:, NSTATE:],
        neg,
        mixed_in,
        z_gate[0, 0],
        skip_gain[None, :],
        out_w,
    )
    parts = 2
    part = width // parts
    sums = []
    for k in range(parts):
        cols = slice(k * part, (k + 1) * part)
        blocks = add_up(kept[:, cols], swap_pair(sent[:, cols])).reshape(line, row_count, part)
        sums.append(line_sum(blocks, place))
    mixer_out = jnp.concatenate(sums, axis=1)

    stream_f = (residual[0, 0].astype(F32) + mixer_out).astype(BF16).astype(F32)
    normed = (
        stream_f
        * lax.rsqrt(jnp.mean(stream_f * stream_f, axis=1, keepdims=True) + 1e-05)
        * norm_gain[None, :]
    ).astype(BF16)
    ids, weights = route_ids[0, 0], route_w[0, 0]
    capacity = min(row_count, 8 * ((3 * row_count * TOP + 16 * line - 1) // (16 * line)))
    named = jnp.any(ids[:, :, None] == jnp.arange(line, dtype=jnp.int32), axis=1)
    rank = jnp.cumsum(named.astype(jnp.int32), axis=0) - 1
    rank_of = jnp.take_along_axis(rank, ids, axis=1)
    slots = jnp.arange(line * capacity, dtype=jnp.int32)
    slot_of = ids * capacity + rank_of
    placing = jnp.any(slot_of[:, :, None] == slots, axis=1).astype(BF16)
    packed = lax.dot_general(
        placing, normed, (((0,), (0,)), ((), ())), preferred_element_type=F32
    ).astype(BF16)
    groups = [[2 * i + o for i in range(line)] for o in range(2)]
    own = lax.all_to_all(
        packed, "expert", split_axis=0, concat_axis=0, axis_index_groups=groups, tiled=True
    )
    rows = line * capacity
    cut = rows // 2
    far_dp = range(1, dps)
    from_y = swap_pair(own)
    from_x = [shift(own, "dp", s) for s in far_dp]
    diagonal = [
        (shift(from_y[:cut], "dp", s), swap_pair(from_x[s - 1][cut:])) for s in far_dp
    ]

    def all_cores(pieces):
        return pieces + [shift(p, "context", s) for s in range(1, contexts) for p in pieces]

    hidden = []
    for pieces in ([own], [from_y] + from_x, [p for pair in diagonal for p in pair]):
        hidden.append(gate_up(all_cores(pieces), w_gate[0], w_up[0]))
    near = 2 * dps * rows
    places = []
    for core in range(contexts):
        base = core * near
        places.append((0, core * rows, base, rows))
        places.append((1, core * dps * rows, base + rows, dps * rows))
        places.append((2, core * (dps - 1) * rows, base + (dps + 1) * rows, (dps - 1) * rows))

    back = []
    for k in range(parts):
        out, far = down(hidden, places, near, w_down[0], k * part, part)
        for s in range(1, contexts):
            got = shift(far[(s - 1) * near : s * near], "context", -s)
            out = add_up(out, got)
        blocks = out.astype(BF16).reshape(2 * dps, rows, part)
        mid = part // 2
        own_sum = blocks[0]
        by_y, by_x, by_both = blocks[1], blocks[2 : dps + 1], blocks[dps + 1 :]
        y_left = add_up(by_y[:, :mid], *[shift(by_both[s - 1, :, :mid], "dp", -s) for s in far_dp])
        y_all = jnp.concatenate([y_left.astype(BF16), by_y[:, mid:]], axis=1)
        x_right = add_up(by_x[:, :, mid:], swap_pair(by_both[:, :, mid:])).astype(BF16)
        x_all = jnp.concatenate([by_x[:, :, :mid], x_right], axis=2)
        total_out = add_up(own_sum, swap_pair(y_all), *[shift(x_all[s - 1], "dp", -s) for s in far_dp])
        outbound = total_out.astype(BF16).reshape(line, capacity, part)
        came = [lax.dynamic_index_in_dim(outbound, place, 0, keepdims=False)]
        for s in range(1, line):
            block = lax.dynamic_index_in_dim(outbound, (place - s) % line, 0, keepdims=False)
            came.append(
                lax.ppermute(block, "expert", [(e, (e - 2 * s) % owners) for e in range(owners)])
            )
        back.append(jnp.concatenate(came, axis=0))
    slot_here = ((ids - place) % line) * capacity + rank_of
    weighting = jnp.sum(
        jnp.where(slot_here[:, :, None] == slots, weights[:, :, None], 0.0), axis=1
    )
    expert_sum = jnp.concatenate(
        [
            jnp.dot(
                weighting, b.astype(F32), precision=lax.Precision.HIGHEST, preferred_element_type=F32
            )
            for b in back
        ],
        axis=1,
    )
    mixed = (stream_f + expert_sum).astype(BF16)
    return mixed.reshape(1, 1, row_count, width)


def solution(mesh):
    placed = (
        P("dp", "context", "expert", None),
        P("dp", "context", None, "expert"),
        P("dp", "context", None, "expert"),
        P(None, "expert"),
        P("expert"),
        P("expert", None),
        P(None, "expert"),
        P("expert"),
        P(None, "expert"),
        P("expert"),
        P("expert", None),
        P(),
        P("dp", "context", "expert", None),
        P("dp", "context", "expert", None),
        P("expert", None, ("context", "dp")),
        P("expert", None, ("context", "dp")),
        P("expert", ("context", "dp"), None),
    )
    return jax.shard_map(
        on_device,
        mesh=mesh,
        in_specs=placed,
        out_specs=P("dp", "context", "expert", None),
        check_vma=False,
    )
```

time: 577 us -> 265 us (0.46)
  waiting for transfers between devices: 279 us -> 77.1 us
  other arithmetic: 130 us -> 9.03 us
  Pallas kernels: 0 us -> 67.4 us
  matrix products: 59.1 us -> 1.37 us
  starting transfers between devices: 8.21 us -> 57.1 us
  local copies, waits for them, and re-layouts: 40.7 us -> 17 us
  between operations: 13.5 us -> 0.98 us
  blocking collectives: 43.2 us -> 33.8 us
    reduce_scatter x2 -> x0, waiting for transfers between devices: 125 us -> none  [the longest x1 66.9 us: on_device(): lax.psum_scatter(partial_out.astype(jnp.bfloat16), 'expert', scatter_dime...]
    reduce_sum x20 -> x1, other arithmetic: 83.6 us -> 0.08 us  [on_device(): jnp.sum(jnp.where(slot_here[:, :, None] == slots, weights[:, :, None], 0....]
    psum x1 -> x0, waiting for transfers between devices: 72 us -> none  [on_device(): lax.psum(jnp.dot(mixed_in, xproj_w, preferred_element_type=jnp.float32).a...]
    ppermute x0 -> x39, waiting for transfers between devices: none -> 69.5 us  [the longest x8 48.3 us: swap_pair(): return lax.ppermute(block, 'expert', [(i, i ^ 1) for i in range(size)])]
    pallas_call x0 -> x7, Pallas kernels: none -> 67.4 us  [the longest x3 38.9 us: gate_up(): pl.pallas_call(functools.partial(gate_up_kernel, len(pieces)), out_shape=...]
    dot_general x6 -> x4, matrix products: 59.1 us -> 1.37 us  [the longest x2 0.57 us: on_device(): jnp.dot(weighting, b.astype(F32), precision=lax.Precision.HIGHEST, prefer...]
    ppermute x0 -> x39, starting transfers between devices: none -> 50 us  [the longest x6 22.4 us: line_sum(): up = lax.ppermute(up.astype(BF16), 'expert', forth[s - 1]).astype(F32)]
    all_gather x1 -> x0, waiting for transfers between devices: 45.2 us -> none  [on_device(): lax.all_gather(flat_rows, ('context', 'dp'), axis=0, tiled=True)]
  transfers between devices with their start and end apart: 6 -> 42, of which waited for: 5 -> 16; matrix products, arithmetic and copies ran while one was open for 0% -> 2% of each run, Pallas kernels for 0% -> 13%
where the time goes in v1:
time: 265 us; the launch traced here: 264 us
  waiting for transfers between devices  77.1 us (29%)
  Pallas kernels  67.4 us (25%)
  starting transfers between devices  57.1 us (22%)
  blocking collectives  33.8 us (13%)
  local copies, waits for them, and re-layouts  17 us (6%)
  other arithmetic  9.03 us (3%)
    ppermute x8, waiting for transfers between devices, swap_pair(): return lax.ppermute(block, 'expert', [(i, i ^ 1) for i in range(size)])  48.3 us
    pallas_call x3, Pallas kernels, gate_up(): pl.pallas_call(functools.partial(gate_up_kernel, len(pieces)), out_shape=...  38.9 us
    ppermute x6, starting transfers between devices, line_sum(): up = lax.ppermute(up.astype(BF16), 'expert', forth[s - 1]).astype(F32)  22.4 us
    all_to_all x1, blocking collectives, on_device(): lax.all_to_all(packed, 'expert', split_axis=0, concat_axis=0, axis_index_...  18.9 us
    all_to_all x1, blocking collectives, on_device(): lax.all_to_all(projected.reshape(owners, length // owners, -1), 'expert',...  14.8 us
    pallas_call x2, Pallas kernels, down(): pl.pallas_call(functools.partial(down_kernel, len(pieces), places), out_s...  14.2 us
    unnamed x51, local copies, waits for them, and re-layouts  12.6 us
    ppermute x13, starting transfers between devices, shift(): lax.ppermute(block, axis, [(i, (i + distance) % size) for i in range(size)])  9.17 us
  transfers between devices with their start and end apart: 42, of which 16 were waited for; matrix products, arithmetic and copies ran while one was open for 2% of the time, Pallas kernels for 13%

profile of v1, /device:TPU:0, one launch (start us, length us, event | category | flops | bytes accessed | tf_op | source)
XLA Modules:
  0.0 263.6 jit_solution(18177952681265877691)
XLA Ops:
  0.8 2.3 collective-permute-start
  6.5 14.8 %all_to_all.21 = bf16[8,32,288]{2,1,0:T(8,128)(2,1)S(1)} all-to-all(bf16[8,32,288]{2,1,0:T(8,128)(2,1)S(1)} %bitcast.177), channel_id=1, replica_groups=mesh['expert'=8,'context'=2,'dp'=2] {'expert'}, dimensions={0} | all-to-all | bytes 294912 | tf_op jit(solution)/shard_map/all_to_all | solution.py:317
  22.1 3.4 %all-to-all-start.1 = ((bf16[8,32,288]{2,1,0:T(8,128)(2,1)}), bf16[8,32,288]{2,1,0:T(8,128)(2,1)S(1)}, u32[]{:S(2)}, u32[]{:S(2)}) async-start(bf16[8,32,288]{2,1,0:T(8,128)(2,1)} %broadcast_in_dim.41), calls=%async_computation.1 | async-start | bytes 393216 | tf_op jit(solution)/shard_map/all_to_all | solution.py:321
  25.6 7.6 %all-to-all-done.1 = bf16[8,32,288]{2,1,0:T(8,128)(2,1)S(1)} async-done(((bf16[8,32,288]{2,1,0:T(8,128)(2,1)}), bf16[8,32,288]{2,1,0:T(8,128)(2,1)S(1)}, u32[]{:S(2)}, u32[]{:S(2)}) %all-to-all-start.1) | async-done | bytes 147488 | tf_op jit(solution)/shard_map/all_to_all | solution.py:321
  34.3 6.4 %state_scan.1 = (f32[2048,128]{1,0:T(8,128)S(1)}, f32[2048,128]{1,0:T(8,128)S(1)}, f32[16,8,128]{2,1,0:T(8,128)S(1)}) custom-call(bf16[256,256]{1,0:T(8,128)(2,1)S(1)} %slice.221.low_ref, bf16[256,32]{1,0:T(8,128)(2,1)S(1)} %slice.222.bc_ref, bf16[256,1024]{1,0:T(8,128)(2,1)S(1)} %copy-done.8, f32[1,1024]{1,0:T(1,128)S(1)} %bitcast.154, ...), custom_call_target="tpu_custom_call" | custom-call | flops 200000000 | bytes 4194304 | tf_op jit(solution)/shard_map/state_scan/pallas_call | solution.py:97
  44.1 3.4 %copy-done.2 = bf16[1024,4096]{1,0:T(8,128)(2,1)S(1)} copy-done((bf16[1024,4096]{1,0:T(8,128)(2,1)S(1)}, bf16[1024,4096]{1,0:T(8,128)(2,1)}, u32[]{:S(2)}) %copy-start.2) | copy-done | bytes 8388632
  48.7 7.9 %readout_project.1 = (bf16[128,4096]{1,0:T(8,128)(2,1)S(1)}, bf16[128,4096]{1,0:T(8,128)(2,1)S(1)}) custom-call(s32[1]{0:T(128)} %bitcast.half_ref, f32[2048,128]{1,0:T(8,128)S(1)} %get-tuple-element.14.y_ref, f32[2048,128]{1,0:T(8,128)S(1)} %copy-done.4, f32[16,8,128]{2,1,0:T(8,128)S(1)} %collective-permute-done.1.enter_ref, ...), custom_call_target="tpu_custom_call" | custom-call | flops 2147483648 | bytes 16777216 | tf_op jit(solution)/shard_map/readout_project/pallas_call | solution.py:161
  59.9 11.6 %collective-permute-done.2 = bf16[128,2048]{1,0:T(8,128)(2,1)S(1)} collective-permute-done((bf16[128,2048]{1,0:T(8,128)(2,1)S(1)}, bf16[128,2048]{1,0:T(8,128)(2,1)S(1)}, u32[]{:S(2)}, u32[]{:S(2)}) %collective-permute-start.2) | collective-permute-done | bytes 524320 | tf_op jit(solution)/shard_map/ppermute | solution.py:34
  71.5 10.5 %collective-permute-done.9 = bf16[128,2048]{1,0:T(8,128)(2,1)S(1)} collective-permute-done((bf16[128,2048]{1,0:T(8,128)(2,1)S(1)}, bf16[128,2048]{1,0:T(8,128)(2,1)S(1)}, u32[]{:S(2)}, u32[]{:S(2)}) %collective-permute-start.9) | collective-permute-done | bytes 524320 | tf_op jit(solution)/shard_map/ppermute | solution.py:34
  82.4 2.1 collective-permute-start.3
  88.1 4.4 %collective-permute-start.4 = (bf16[32,2048]{1,0:T(8,128)(2,1)S(1)}, bf16[32,2048]{1,0:T(8,128)(2,1)S(1)}, u32[]{:S(2)}, u32[]{:S(2)}) collective-permute-start(bf16[32,2048]{1,0:T(8,128)(2,1)S(1)} %get-tuple-element.29), channel_id=1, source_target_pairs={{0,8},{4,12},{8,16},{12,20},{1,9},{5,13},{9,17},{13,21},{2,10},{6,... | collective-permute-start | bytes 393224 | tf_op jit(solution)/shard_map/ppermute | solution.py:271
  93.3 4.2 %collective-permute-start.11 = (bf16[32,2048]{1,0:T(8,128)(2,1)S(1)}, bf16[32,2048]{1,0:T(8,128)(2,1)S(1)}, u32[]{:S(2)}, u32[]{:S(2)}) collective-permute-start(bf16[32,2048]{1,0:T(8,128)(2,1)S(1)} %get-tuple-element.39), channel_id=1, source_target_pairs={{0,8},{4,12},{8,16},{12,20},{1,9},{5,13},{9,17},{13,21},{2,10},{6,... | collective-permute-start | bytes 393224 | tf_op jit(solution)/shard_map/ppermute | solution.py:271
  98.2 5.3 %collective-permute-start.5 = (bf16[32,2048]{1,0:T(8,128)(2,1)S(1)}, bf16[32,2048]{1,0:T(8,128)(2,1)S(1)}, u32[]{:S(2)}, u32[]{:S(2)}) collective-permute-start(bf16[32,2048]{1,0:T(8,128)(2,1)S(1)} %get-tuple-element.27), channel_id=1, source_target_pairs={{0,8},{4,12},{8,16},{12,20},{16,24},{20,28},{1,9},{5,13},{9,17},{1... | collective-permute-start | bytes 393224 | tf_op jit(solution)/shard_map/ppermute | solution.py:271
  105.0 5.2 %collective-permute-start.12 = (bf16[32,2048]{1,0:T(8,128)(2,1)S(1)}, bf16[32,2048]{1,0:T(8,128)(2,1)S(1)}, u32[]{:S(2)}, u32[]{:S(2)}) collective-permute-start(bf16[32,2048]{1,0:T(8,128)(2,1)S(1)} %get-tuple-element.37), channel_id=1, source_target_pairs={{0,8},{4,12},{8,16},{12,20},{16,24},{20,28},{1,9},{5,13},{9,17},{1... | collective-permute-start | bytes 393224 | tf_op jit(solution)/shard_map/ppermute | solution.py:271
  112.6 4.4 %collective-permute-done.15 = bf16[32,2048]{1,0:T(8,128)(2,1)S(1)} collective-permute-done((bf16[32,2048]{1,0:T(8,128)(2,1)S(1)}, bf16[32,2048]{1,0:T(8,128)(2,1)S(1)}, u32[]{:S(2)}, u32[]{:S(2)}) %collective-permute-start.15) | collective-permute-done | bytes 131104 | tf_op jit(solution)/shard_map/ppermute | solution.py:272
  117.7 18.9 %all_to_all.22 = bf16[4,24,4096]{2,1,0:T(8,128)(2,1)S(1)} all-to-all(bf16[4,24,4096]{2,1,0:T(8,128)(2,1)S(1)} %bitcast.171), channel_id=1, replica_groups={{0,8,16,24},{4,12,20,28},{1,9,17,25},{5,13,21,29},{2,10,18,26},{6,14,22..., dimensions={0} | all-to-all | bytes 1572864 | tf_op jit(solution)/shard_map/all_to_all | solution.py:378
  138.3 15.0 %collective-permute-done.17.refs_0_ = bf16[96,4096]{1,0:T(8,128)(2,1)S(1)} collective-permute-done((bf16[96,4096]{1,0:T(8,128)(2,1)S(1)}, bf16[96,4096]{1,0:T(8,128)(2,1)S(1)}, u32[]{:S(2)}, u32[]{:S(2)}) %collective-permute-start.17) | collective-permute-done | bytes 786464 | tf_op jit(solution)/shard_map/ppermute | solution.py:34
  156.8 11.6 %gate_up.3.refs_0_ = bf16[192,1536]{1,0:T(8,128)(2,1)S(1)} custom-call(bf16[96,4096]{1,0:T(8,128)(2,1)S(1)} %bitcast.145, bf16[96,4096]{1,0:T(8,128)(2,1)S(1)} %collective-permute-done.16.refs_1_, bf16[4096,1536]{1,0:T(8,128)(2,1)} %bitcast.155, bf16[4096,1536]{1,0:T(8,128)(2,1)} %bitcast.158), custom_call_target="tpu_custom_call" | custom-call | flops 4831838208 | bytes 26738688 | tf_op jit(solution)/shard_map/gate_up/pallas_call | solution.py:203
  168.9 15.0 %gate_up.4.refs_1_ = bf16[384,1536]{1,0:T(8,128)(2,1)S(1)} custom-call(bf16[96,4096]{1,0:T(8,128)(2,1)S(1)} %collective-permute-done.17.refs_0_, bf16[96,4096]{1,0:T(8,128)(2,1)S(1)} %collective-permute-done.18.refs_1_, bf16[96,4096]{1,0:T(8,128)(2,1)S(1)} %collective-permute-done.19.refs_2_, bf16[96,4096]{1,0:T(8,128)(2,1)S(1)} %collective-permute-done.20.refs_3_, ...), custom_call_target="tpu_custom_call" | custom-call | flops 9663676416 | bytes 28311552 | tf_op jit(solution)/shard_map/gate_up/pallas_call | solution.py:203
  184.0 12.3 %gate_up.5.refs_2_ = bf16[192,1536]{1,0:T(8,128)(2,1)S(1)} custom-call(bf16[48,4096]{1,0:T(8,128)(2,1)S(1)} %collective-permute-done.21.refs_0_, bf16[48,4096]{1,0:T(8,128)(2,1)S(1)} %collective-permute-done.22.refs_1_, bf16[48,4096]{1,0:T(8,128)(2,1)S(1)} %collective-permute-done.23.refs_2_, bf16[48,4096]{1,0:T(8,128)(2,1)S(1)} %collective-permute-done.24.refs_3_, ...), custom_call_target="tpu_custom_call" | custom-call | flops 4831838208 | bytes 26738688 | tf_op jit(solution)/shard_map/gate_up/pallas_call | solution.py:203
  196.4 7.1 %down.2 = (bf16[384,2048]{1,0:T(8,128)(2,1)S(1)}, bf16[384,2048]{1,0:T(8,128)(2,1)}) custom-call(bf16[192,1536]{1,0:T(8,128)(2,1)S(1)} %gate_up.3.refs_0_, bf16[384,1536]{1,0:T(8,128)(2,1)S(1)} %gate_up.4.refs_1_, bf16[192,1536]{1,0:T(8,128)(2,1)S(1)} %gate_up.5.refs_2_, bf16[1536,4096]{1,0:T(8,128)(2,1)S(1)} %bitcast.152), custom_call_target="tpu_custom_call" | custom-call | flops 4831838208 | bytes 11796480 | tf_op jit(solution)/shard_map/down/pallas_call | solution.py:236
  203.6 4.6 %copy-done.7 = bf16[1,1536,4096]{2,1,0:T(8,128)(2,1)S(1)} copy-done((bf16[1,1536,4096]{2,1,0:T(8,128)(2,1)S(1)}, bf16[1,1536,4096]{2,1,0:T(8,128)(2,1)}, u32[]{:S(2)}) %copy-start.7) | copy-done | bytes 12582936
  209.4 7.1 %down.3 = (bf16[384,2048]{1,0:T(8,128)(2,1)S(1)}, bf16[384,2048]{1,0:T(8,128)(2,1)}) custom-call(bf16[192,1536]{1,0:T(8,128)(2,1)S(1)} %gate_up.3.refs_0_, bf16[384,1536]{1,0:T(8,128)(2,1)S(1)} %copy-done.11, bf16[192,1536]{1,0:T(8,128)(2,1)S(1)} %gate_up.5.refs_2_, bf16[1536,4096]{1,0:T(8,128)(2,1)S(1)} %bitcast.153), custom_call_target="tpu_custom_call" | custom-call | flops 4831838208 | bytes 11796480 | tf_op jit(solution)/shard_map/down/pallas_call | solution.py:236
  217.1 2.0 add_convert_fusion.1
  220.3 2.0 add_convert_fusion
  226.7 3.5 %collective-permute-done.26 = bf16[96,1024]{1,0:T(8,128)(2,1)S(1)} collective-permute-done((bf16[96,1024]{1,0:T(8,128)(2,1)S(1)}, bf16[96,1024]{1,0:T(8,128)(2,1)S(1)}, u32[]{:S(2)}, u32[]{:S(2)}) %collective-permute-start.26) | collective-permute-done | bytes 196640 | tf_op jit(solution)/shard_map/ppermute | solution.py:29
  232.5 2.0 collective-permute-done.34
  236.7 6.8 %collective-permute-done.27 = bf16[96,2048]{1,0:T(8,128)(2,1)S(1)} collective-permute-done((bf16[96,2048]{1,0:T(8,128)(2,1)S(1)}, bf16[96,2048]{1,0:T(8,128)(2,1)S(1)}, u32[]{:S(2)}, u32[]{:S(2)}) %collective-permute-start.27) | collective-permute-done | bytes 393248 | tf_op jit(solution)/shard_map/ppermute | solution.py:34
  243.7 2.3 collective-permute-start.30
  246.6 4.4 %collective-permute-done.35 = bf16[96,2048]{1,0:T(8,128)(2,1)S(1)} collective-permute-done((bf16[96,2048]{1,0:T(8,128)(2,1)S(1)}, bf16[96,2048]{1,0:T(8,128)(2,1)S(1)}, u32[]{:S(2)}, u32[]{:S(2)}) %collective-permute-start.35) | collective-permute-done | bytes 393248 | tf_op jit(solution)/shard_map/ppermute | solution.py:34
  251.2 2.3 collective-permute-start.38
  256.8 5.8 %collective-permute-done.39 = bf16[24,2048]{1,0:T(8,128)(2,1)S(1)} collective-permute-done((bf16[24,2048]{1,0:T(8,128)(2,1)S(1)}, bf16[24,2048]{1,0:T(8,128)(2,1)S(1)}, u32[]{:S(2)}, u32[]{:S(2)}) %collective-permute-start.39) | collective-permute-done | bytes 98336 | tf_op jit(solution)/shard_map/ppermute | solution.py:424
  (179 shorter events, 46.6 us)
Async XLA Ops:
  22.1 11.1 %all-to-all-start.1 = ((bf16[8,32,288]{2,1,0:T(8,128)(2,1)}), bf16[8,32,288]{2,1,0:T(8,128)(2,1)S(1)}, u32[]{:S(2)}, u32[]{:S(2)}) async-start(bf16[8,32,288]{2,1,0:T(8,128)(2,1)} %broadcast_in_dim.41), calls=%async_computation.1 | async-start | bytes 393216 | tf_op jit(solution)/shard_map/all_to_all | solution.py:321
  56.7 14.8 %collective-permute-start.2 = (bf16[128,2048]{1,0:T(8,128)(2,1)S(1)}, bf16[128,2048]{1,0:T(8,128)(2,1)S(1)}, u32[]{:S(2)}, u32[]{:S(2)}) collective-permute-start(bf16[128,2048]{1,0:T(8,128)(2,1)S(1)} %get-tuple-element.35), channel_id=1, source_target_pairs={{0,4},{4,0},{8,12},{12,8},{16,20},{20,16},{24,28},{28,24},{1,5},{5... | collective-permute-start | bytes 1572872 | tf_op jit(solution)/shard_map/ppermute | solution.py:34
  57.7 24.3 %collective-permute-start.9 = (bf16[128,2048]{1,0:T(8,128)(2,1)S(1)}, bf16[128,2048]{1,0:T(8,128)(2,1)S(1)}, u32[]{:S(2)}, u32[]{:S(2)}) collective-permute-start(bf16[128,2048]{1,0:T(8,128)(2,1)S(1)} %get-tuple-element.36), channel_id=1, source_target_pairs={{0,4},{4,0},{8,12},{12,8},{16,20},{20,16},{24,28},{28,24},{1,5},{5... | collective-permute-start | bytes 1572872 | tf_op jit(solution)/shard_map/ppermute | solution.py:34
  85.2 8.0 %collective-permute-start.10 = (bf16[32,2048]{1,0:T(8,128)(2,1)S(1)}, bf16[32,2048]{1,0:T(8,128)(2,1)S(1)}, u32[]{:S(2)}, u32[]{:S(2)}) collective-permute-start(bf16[32,2048]{1,0:T(8,128)(2,1)S(1)} %get-tuple-element.41), channel_id=1, source_target_pairs={{0,8},{4,12},{1,9},{5,13},{2,10},{6,14},{3,11},{7,15}} | collective-permute-start | bytes 393224 | tf_op jit(solution)/shard_map/ppermute | solution.py:271
  88.1 10.0 %collective-permute-start.4 = (bf16[32,2048]{1,0:T(8,128)(2,1)S(1)}, bf16[32,2048]{1,0:T(8,128)(2,1)S(1)}, u32[]{:S(2)}, u32[]{:S(2)}) collective-permute-start(bf16[32,2048]{1,0:T(8,128)(2,1)S(1)} %get-tuple-element.29), channel_id=1, source_target_pairs={{0,8},{4,12},{8,16},{12,20},{1,9},{5,13},{9,17},{13,21},{2,10},{6,... | collective-permute-start | bytes 393224 | tf_op jit(solution)/shard_map/ppermute | solution.py:271
  93.3 11.6 %collective-permute-start.11 = (bf16[32,2048]{1,0:T(8,128)(2,1)S(1)}, bf16[32,2048]{1,0:T(8,128)(2,1)S(1)}, u32[]{:S(2)}, u32[]{:S(2)}) collective-permute-start(bf16[32,2048]{1,0:T(8,128)(2,1)S(1)} %get-tuple-element.39), channel_id=1, source_target_pairs={{0,8},{4,12},{8,16},{12,20},{1,9},{5,13},{9,17},{13,21},{2,10},{6,... | collective-permute-start | bytes 393224 | tf_op jit(solution)/shard_map/ppermute | solution.py:271
  98.2 13.2 %collective-permute-start.5 = (bf16[32,2048]{1,0:T(8,128)(2,1)S(1)}, bf16[32,2048]{1,0:T(8,128)(2,1)S(1)}, u32[]{:S(2)}, u32[]{:S(2)}) collective-permute-start(bf16[32,2048]{1,0:T(8,128)(2,1)S(1)} %get-tuple-element.27), channel_id=1, source_target_pairs={{0,8},{4,12},{8,16},{12,20},{16,24},{20,28},{1,9},{5,13},{9,17},{1... | collective-permute-start | bytes 393224 | tf_op jit(solution)/shard_map/ppermute | solution.py:271
  103.6 8.6 %collective-permute-start.8 = (bf16[32,2048]{1,0:T(8,128)(2,1)S(1)}, bf16[32,2048]{1,0:T(8,128)(2,1)S(1)}, u32[]{:S(2)}, u32[]{:S(2)}) collective-permute-start(bf16[32,2048]{1,0:T(8,128)(2,1)S(1)} %get-tuple-element.28), channel_id=1, source_target_pairs={{8,0},{12,4},{16,8},{20,12},{24,16},{28,20},{9,1},{13,5},{17,9},{2... | collective-permute-start | bytes 393224 | tf_op jit(solution)/shard_map/ppermute | solution.py:272
  105.0 7.7 %collective-permute-start.12 = (bf16[32,2048]{1,0:T(8,128)(2,1)S(1)}, bf16[32,2048]{1,0:T(8,128)(2,1)S(1)}, u32[]{:S(2)}, u32[]{:S(2)}) collective-permute-start(bf16[32,2048]{1,0:T(8,128)(2,1)S(1)} %get-tuple-element.37), channel_id=1, source_target_pairs={{0,8},{4,12},{8,16},{12,20},{16,24},{20,28},{1,9},{5,13},{9,17},{1... | collective-permute-start | bytes 393224 | tf_op jit(solution)/shard_map/ppermute | solution.py:271
  136.6 16.7 %collective-permute-start.17 = (bf16[96,4096]{1,0:T(8,128)(2,1)S(1)}, bf16[96,4096]{1,0:T(8,128)(2,1)S(1)}, u32[]{:S(2)}, u32[]{:S(2)}) collective-permute-start(bf16[96,4096]{1,0:T(8,128)(2,1)S(1)} %bitcast.142), channel_id=1, source_target_pairs={{0,4},{4,0},{8,12},{12,8},{16,20},{20,16},{24,28},{28,24},{1,5},{5... | collective-permute-start | bytes 2359304 | tf_op jit(solution)/shard_map/ppermute | solution.py:34
  136.8 16.5 %collective-permute-start.18 = (bf16[96,4096]{1,0:T(8,128)(2,1)S(1)}, bf16[96,4096]{1,0:T(8,128)(2,1)S(1)}, u32[]{:S(2)}, u32[]{:S(2)}) collective-permute-start(bf16[96,4096]{1,0:T(8,128)(2,1)S(1)} %bitcast.143), channel_id=1, source_target_pairs={{0,1},{1,0},{2,3},{3,2},{4,5},{5,4},{6,7},{7,6},{8,9},{9,8},{10,11... | collective-permute-start | bytes 2359304 | tf_op jit(solution)/shard_map/ppermute | solution.py:29
  138.3 18.5 %collective-permute-start.16 = (bf16[96,4096]{1,0:T(8,128)(2,1)S(1)}, bf16[96,4096]{1,0:T(8,128)(2,1)S(1)}, u32[]{:S(2)}, u32[]{:S(2)}) collective-permute-start(bf16[96,4096]{1,0:T(8,128)(2,1)S(1)} %bitcast.144), channel_id=1, source_target_pairs={{0,2},{2,0},{1,3},{3,1},{4,6},{6,4},{5,7},{7,5},{8,10},{10,8},{9,1... | collective-permute-start | bytes 2359304 | tf_op jit(solution)/shard_map/ppermute | solution.py:29
  153.3 15.6 %collective-permute-start.19 = (bf16[96,4096]{1,0:T(8,128)(2,1)S(1)}, bf16[96,4096]{1,0:T(8,128)(2,1)S(1)}, u32[]{:S(2)}, u32[]{:S(2)}) collective-permute-start(bf16[96,4096]{1,0:T(8,128)(2,1)S(1)} %collective-permute-done.17.refs_0_), channel_id=1, source_target_pairs={{0,2},{2,0},{1,3},{3,1},{4,6},{6,4},{5,7},{7,5},{8,10},{10,8},{9,1... | collective-permute-start | bytes 2359304 | tf_op jit(solution)/shard_map/ppermute | solution.py:29
  153.3 15.6 %collective-permute-start.20 = (bf16[96,4096]{1,0:T(8,128)(2,1)S(1)}, bf16[96,4096]{1,0:T(8,128)(2,1)S(1)}, u32[]{:S(2)}, u32[]{:S(2)}) collective-permute-start(bf16[96,4096]{1,0:T(8,128)(2,1)S(1)} %collective-permute-done.18.refs_1_), channel_id=1, source_target_pairs={{0,2},{2,0},{1,3},{3,1},{4,6},{6,4},{5,7},{7,5},{8,10},{10,8},{9,1... | collective-permute-start | bytes 2359304 | tf_op jit(solution)/shard_map/ppermute | solution.py:29
  153.9 14.5 %collective-permute-start.21 = (bf16[48,4096]{1,0:T(8,128)(2,1)S(1)}, bf16[48,4096]{1,0:T(8,128)(2,1)S(1)}, u32[]{:S(2)}, u32[]{:S(2)}) collective-permute-start(bf16[48,4096]{1,0:T(8,128)(2,1)S(1)} %slice.224), channel_id=1, source_target_pairs={{0,1},{1,0},{2,3},{3,2},{4,5},{5,4},{6,7},{7,6},{8,9},{9,8},{10,11... | collective-permute-start | bytes 1179656 | tf_op jit(solution)/shard_map/ppermute | solution.py:29
  155.5 13.0 %collective-permute-start.22 = (bf16[48,4096]{1,0:T(8,128)(2,1)S(1)}, bf16[48,4096]{1,0:T(8,128)(2,1)S(1)}, u32[]{:S(2)}, u32[]{:S(2)}) collective-permute-start(bf16[48,4096]{1,0:T(8,128)(2,1)S(1)} %slice.225), channel_id=1, source_target_pairs={{0,4},{4,0},{8,12},{12,8},{16,20},{20,16},{24,28},{28,24},{1,5},{5... | collective-permute-start | bytes 1179656 | tf_op jit(solution)/shard_map/ppermute | solution.py:34
  168.3 15.7 %collective-permute-start.23 = (bf16[48,4096]{1,0:T(8,128)(2,1)S(1)}, bf16[48,4096]{1,0:T(8,128)(2,1)S(1)}, u32[]{:S(2)}, u32[]{:S(2)}) collective-permute-start(bf16[48,4096]{1,0:T(8,128)(2,1)S(1)} %collective-permute-done.21.refs_0_), channel_id=1, source_target_pairs={{0,2},{2,0},{1,3},{3,1},{4,6},{6,4},{5,7},{7,5},{8,10},{10,8},{9,1... | collective-permute-start | bytes 1179656 | tf_op jit(solution)/shard_map/ppermute | solution.py:29
  168.4 15.6 %collective-permute-start.24 = (bf16[48,4096]{1,0:T(8,128)(2,1)S(1)}, bf16[48,4096]{1,0:T(8,128)(2,1)S(1)}, u32[]{:S(2)}, u32[]{:S(2)}) collective-permute-start(bf16[48,4096]{1,0:T(8,128)(2,1)S(1)} %collective-permute-done.22.refs_1_), channel_id=1, source_target_pairs={{0,2},{2,0},{1,3},{3,1},{4,6},{6,4},{5,7},{7,5},{8,10},{10,8},{9,1... | collective-permute-start | bytes 1179656 | tf_op jit(solution)/shard_map/ppermute | solution.py:29
  203.5 13.5 %collective-permute-start.25 = (bf16[384,2048]{1,0:T(8,128)(2,1)}, bf16[384,2048]{1,0:T(8,128)(2,1)}, u32[]{:S(2)}, u32[]{:S(2)}) collective-permute-start(bf16[384,2048]{1,0:T(8,128)(2,1)} %get-tuple-element.20), channel_id=1, source_target_pairs={{0,2},{2,0},{1,3},{3,1},{4,6},{6,4},{5,7},{7,5},{8,10},{10,8},{9,1... | collective-permute-start | bytes 4718600 | tf_op jit(solution)/shard_map/ppermute | solution.py:29
  222.5 7.8 %collective-permute-start.26 = (bf16[96,1024]{1,0:T(8,128)(2,1)S(1)}, bf16[96,1024]{1,0:T(8,128)(2,1)S(1)}, u32[]{:S(2)}, u32[]{:S(2)}) collective-permute-start(bf16[96,1024]{1,0:T(8,128)(2,1)S(1)} %get-tuple-element.47), channel_id=1, source_target_pairs={{0,1},{1,0},{2,3},{3,2},{4,5},{5,4},{6,7},{7,6},{8,9},{9,8},{10,11... | collective-permute-start | bytes 589832 | tf_op jit(solution)/shard_map/ppermute | solution.py:29
  223.1 8.1 %collective-permute-start.28 = (bf16[1,96,1024]{2,1,0:T(8,128)(2,1)S(1)}, bf16[1,96,1024]{2,1,0:T(8,128)(2,1)S(1)}, u32[]{:S(2)}, u32[]{:S(2)}) collective-permute-start(bf16[1,96,1024]{2,1,0:T(8,128)(2,1)S(1)} %get-tuple-element.48), channel_id=1, source_target_pairs={{0,4},{4,0},{8,12},{12,8},{16,20},{20,16},{24,28},{28,24},{1,5},{5... | collective-permute-start | bytes 589832 | tf_op jit(solution)/shard_map/ppermute | solution.py:34
  223.9 10.6 %collective-permute-start.34 = (bf16[96,1024]{1,0:T(8,128)(2,1)S(1)}, bf16[96,1024]{1,0:T(8,128)(2,1)S(1)}, u32[]{:S(2)}, u32[]{:S(2)}) collective-permute-start(bf16[96,1024]{1,0:T(8,128)(2,1)S(1)} %get-tuple-element.53), channel_id=1, source_target_pairs={{0,1},{1,0},{2,3},{3,2},{4,5},{5,4},{6,7},{7,6},{8,9},{9,8},{10,11... | collective-permute-start | bytes 589832 | tf_op jit(solution)/shard_map/ppermute | solution.py:29
  225.5 9.9 %collective-permute-start.36 = (bf16[1,96,1024]{2,1,0:T(8,128)(2,1)S(1)}, bf16[1,96,1024]{2,1,0:T(8,128)(2,1)S(1)}, u32[]{:S(2)}, u32[]{:S(2)}) collective-permute-start(bf16[1,96,1024]{2,1,0:T(8,128)(2,1)S(1)} %get-tuple-element.54), channel_id=1, source_target_pairs={{0,4},{4,0},{8,12},{12,8},{16,20},{20,16},{24,28},{28,24},{1,5},{5... | collective-permute-start | bytes 589832 | tf_op jit(solution)/shard_map/ppermute | solution.py:34
  230.3 13.1 %collective-permute-start.27 = (bf16[96,2048]{1,0:T(8,128)(2,1)S(1)}, bf16[96,2048]{1,0:T(8,128)(2,1)S(1)}, u32[]{:S(2)}, u32[]{:S(2)}) collective-permute-start(bf16[96,2048]{1,0:T(8,128)(2,1)S(1)} %pad_maximum_fusion), channel_id=1, source_target_pairs={{0,4},{4,0},{8,12},{12,8},{16,20},{20,16},{24,28},{28,24},{1,5},{5... | collective-permute-start | bytes 1179656 | tf_op jit(solution)/shard_map/ppermute | solution.py:34
  231.3 12.2 %collective-permute-start.29 = (bf16[96,2048]{1,0:T(8,128)(2,1)S(1)}, bf16[96,2048]{1,0:T(8,128)(2,1)S(1)}, u32[]{:S(2)}, u32[]{:S(2)}) collective-permute-start(bf16[96,2048]{1,0:T(8,128)(2,1)S(1)} %maximum_bitcast_fusion), channel_id=1, source_target_pairs={{0,1},{1,0},{2,3},{3,2},{4,5},{5,4},{6,7},{7,6},{8,9},{9,8},{10,11... | collective-permute-start | bytes 1179656 | tf_op jit(solution)/shard_map/ppermute | solution.py:29
  234.6 16.5 %collective-permute-start.35 = (bf16[96,2048]{1,0:T(8,128)(2,1)S(1)}, bf16[96,2048]{1,0:T(8,128)(2,1)S(1)}, u32[]{:S(2)}, u32[]{:S(2)}) collective-permute-start(bf16[96,2048]{1,0:T(8,128)(2,1)S(1)} %pad_maximum_fusion.1), channel_id=1, source_target_pairs={{0,4},{4,0},{8,12},{12,8},{16,20},{20,16},{24,28},{28,24},{1,5},{5... | collective-permute-start | bytes 1179656 | tf_op jit(solution)/shard_map/ppermute | solution.py:34
  235.5 15.5 %collective-permute-start.37 = (bf16[96,2048]{1,0:T(8,128)(2,1)S(1)}, bf16[96,2048]{1,0:T(8,128)(2,1)S(1)}, u32[]{:S(2)}, u32[]{:S(2)}) collective-permute-start(bf16[96,2048]{1,0:T(8,128)(2,1)S(1)} %maximum_bitcast_fusion.1), channel_id=1, source_target_pairs={{0,1},{1,0},{2,3},{3,2},{4,5},{5,4},{6,7},{7,6},{8,9},{9,8},{10,11... | collective-permute-start | bytes 1179656 | tf_op jit(solution)/shard_map/ppermute | solution.py:29
  243.7 9.9 %collective-permute-start.30 = (bf16[24,2048]{1,0:T(8,128)(2,1)S(1)}, bf16[24,2048]{1,0:T(8,128)(2,1)S(1)}, u32[]{:S(2)}, u32[]{:S(2)}) collective-permute-start(bf16[24,2048]{1,0:T(8,128)(2,1)S(1)} %get-tuple-element.46), channel_id=1, source_target_pairs={{0,24},{4,28},{8,0},{12,4},{16,8},{20,12},{24,16},{28,20},{1,25},{... | collective-permute-start | bytes 294920 | tf_op jit(solution)/shard_map/ppermute | solution.py:424
  246.0 9.1 %collective-permute-start.31 = (bf16[24,2048]{1,0:T(8,128)(2,1)S(1)}, bf16[24,2048]{1,0:T(8,128)(2,1)S(1)}, u32[]{:S(2)}, u32[]{:S(2)}) collective-permute-start(bf16[24,2048]{1,0:T(8,128)(2,1)S(1)} %get-tuple-element.45), channel_id=1, source_target_pairs={{0,16},{4,20},{8,24},{12,28},{16,0},{20,4},{24,8},{28,12},{1,17},{... | collective-permute-start | bytes 294920 | tf_op jit(solution)/shard_map/ppermute | solution.py:424
  246.0 9.1 %collective-permute-start.32 = (bf16[24,2048]{1,0:T(8,128)(2,1)S(1)}, bf16[24,2048]{1,0:T(8,128)(2,1)S(1)}, u32[]{:S(2)}, u32[]{:S(2)}) collective-permute-start(bf16[24,2048]{1,0:T(8,128)(2,1)S(1)} %get-tuple-element.44), channel_id=1, source_target_pairs={{0,8},{4,12},{8,16},{12,20},{16,24},{20,28},{24,0},{28,4},{1,9},{5... | collective-permute-start | bytes 294920 | tf_op jit(solution)/shard_map/ppermute | solution.py:424
  253.6 9.0 %collective-permute-start.39 = (bf16[24,2048]{1,0:T(8,128)(2,1)S(1)}, bf16[24,2048]{1,0:T(8,128)(2,1)S(1)}, u32[]{:S(2)}, u32[]{:S(2)}) collective-permute-start(bf16[24,2048]{1,0:T(8,128)(2,1)S(1)} %get-tuple-element.51), channel_id=1, source_target_pairs={{0,16},{4,20},{8,24},{12,28},{16,0},{20,4},{24,8},{28,12},{1,17},{... | collective-permute-start | bytes 294920 | tf_op jit(solution)/shard_map/ppermute | solution.py:424
  253.6 9.0 %collective-permute-start.40 = (bf16[24,2048]{1,0:T(8,128)(2,1)S(1)}, bf16[24,2048]{1,0:T(8,128)(2,1)S(1)}, u32[]{:S(2)}, u32[]{:S(2)}) collective-permute-start(bf16[24,2048]{1,0:T(8,128)(2,1)S(1)} %get-tuple-element.50), channel_id=1, source_target_pairs={{0,8},{4,12},{8,16},{12,20},{16,24},{20,28},{24,0},{28,4},{1,9},{5... | collective-permute-start | bytes 294920 | tf_op jit(solution)/shard_map/ppermute | solution.py:424
  (35 other events, 333.9 us)

commit v2 on v1

v2 whole, which is shorter than its diff:
```python
import functools

import jax
import jax.numpy as jnp
from jax import lax
from jax.experimental import pallas as pl
from jax.experimental.pallas import tpu as pltpu
from jax.sharding import PartitionSpec as P

NSTATE = 16
DT_RANK = 256
CONV = 4
TOP = 2
LANES = 128
SUB = 8
F32 = jnp.float32
BF16 = jnp.bfloat16
MIB = 1 << 20


def from_behind(block, axis, distance):
    devices = range(lax.axis_size(axis))
    route = [(i - distance, i) for i in devices if i - distance in devices]
    return lax.ppermute(block, axis, route)


def shift(block, axis, distance):
    size = lax.axis_size(axis)
    return lax.ppermute(block, axis, [(i, (i + distance) % size) for i in range(size)])


def swap_pair(block):
    size = lax.axis_size("expert")
    return lax.ppermute(block, "expert", [(i, i ^ 1) for i in range(size)])


def cost(flops, bytes_accessed, transcendentals=0):
    return pl.CostEstimate(
        flops=int(flops), bytes_accessed=int(bytes_accessed), transcendentals=int(transcendentals)
    )


def spread_rows(values, wide_ref):
    length, count = values.shape
    col = lax.broadcasted_iota(jnp.int32, (count, count * LANES), 1)
    row = lax.broadcasted_iota(jnp.int32, (count, count * LANES), 0)
    ones = jnp.where((col >= row * LANES) & (col < (row + 1) * LANES), 1.0, 0.0).astype(BF16)
    out = jnp.dot(values, ones, preferred_element_type=F32)
    for n in range(count):
        wide_ref[pl.ds(n * length, length), :] = out[:, n * LANES : (n + 1) * LANES]


def scan_kernel(groups, line, place_ref, *refs):
    pieces, refs = refs[:line], refs[line:]
    w_ref, bias_ref, neg_ref, x_ref, y_ref, sum_ref, end_ref, bc_ref = refs[:8]
    low_ref, step_ref, drive_ref, wide_ref = refs[8:]
    length = x_ref.shape[0]
    share = length // line
    for s in range(line):
        start = pl.multiple_of((place_ref[0] + (line - s)) % line * share, share)
        low_ref[pl.ds(start, share), :] = pieces[s][:, :DT_RANK]
        bc_ref[pl.ds(start, share), :] = pieces[s][:, DT_RANK:]
    spread_rows(bc_ref[...], wide_ref)
    for g in range(SUB):
        rows = pl.ds(g, length, stride=SUB)
        if g >= groups:
            step_ref[rows, :] = jnp.zeros((length, LANES), F32)
            drive_ref[rows, :] = jnp.zeros((length, LANES), F32)
            continue
        cols = pl.ds(g * LANES, LANES)
        raw = jnp.dot(low_ref[...], w_ref[:, cols], preferred_element_type=F32) + bias_ref[:, cols]
        step = jnp.maximum(raw, 0.0) + jnp.log1p(jnp.exp(-jnp.abs(raw)))
        step_ref[rows, :] = step
        drive_ref[rows, :] = step * x_ref[:, cols].astype(F32)

    def block(k, carry):
        states, total = list(carry[0]), carry[1]
        for u in range(SUB):
            t = k * SUB + u
            here = pl.ds(pl.multiple_of(t * SUB, SUB), SUB)
            step, drive = step_ref[here, :], drive_ref[here, :]
            total = total + step
            out = jnp.zeros((SUB, LANES), F32)
            for n in range(NSTATE):
                decay = jnp.exp(step * neg_ref[n])
                b = wide_ref[pl.ds(n * length + t, 1), :]
                c = wide_ref[pl.ds((NSTATE + n) * length + t, 1), :]
                states[n] = states[n] * decay + drive * b
                out = out + states[n] * c
            y_ref[here, :] = out
            sum_ref[here, :] = total
        return tuple(states), total

    zero = jnp.zeros((SUB, LANES), F32)
    states, total = lax.fori_loop(0, length // SUB, block, ((zero,) * NSTATE, zero))
    for n in range(NSTATE):
        end_ref[n] = states[n]


def run_scan(place, pieces, w, bias, neg, x):
    length, channels = x.shape
    vmem = pl.BlockSpec(memory_space=pltpu.VMEM)
    tall = jax.ShapeDtypeStruct((length * SUB, LANES), F32)
    return pl.pallas_call(
        functools.partial(scan_kernel, channels // LANES, len(pieces)),
        out_shape=(
            tall,
            tall,
            jax.ShapeDtypeStruct((NSTATE, SUB, LANES), F32),
            jax.ShapeDtypeStruct((length, 2 * NSTATE), BF16),
        ),
        in_specs=[pl.BlockSpec(memory_space=pltpu.SMEM)] + [vmem] * (len(pieces) + 4),
        out_specs=(vmem,) * 4,
        scratch_shapes=[
            pltpu.VMEM((length, DT_RANK), BF16),
            pltpu.VMEM((length * SUB, LANES), F32),
            pltpu.VMEM((length * SUB, LANES), F32),
            pltpu.VMEM((2 * NSTATE * length, LANES), F32),
        ],
        compiler_params=pltpu.CompilerParams(vmem_limit_bytes=20 * MIB),
        cost_estimate=cost(2e8, 4 * MIB, NSTATE * length * channels),
        name="state_scan",
    )(place, *pieces, w, bias, neg, x)


def out_kernel(groups, line, parts, at_ref, y_ref, sum_ref, enter_ref, bc_ref, neg_ref, x_ref, z_ref,
               skip_ref, w_ref, *refs):
    kept_refs, sent_refs = refs[:parts], refs[parts : 2 * parts]
    full_ref, wide_ref, gated_ref, order_ref = refs[2 * parts :]
    length = x_ref.shape[0]
    spread_rows(bc_ref[:, NSTATE:], wide_ref)

    def block(k, carry):
        for u in range(SUB):
            t = k * SUB + u
            here = pl.ds(pl.multiple_of(t * SUB, SUB), SUB)
            total = sum_ref[here, :]
            out = y_ref[here, :]
            for n in range(NSTATE):
                c = wide_ref[pl.ds(n * length + t, 1), :]
                out = out + jnp.exp(total * neg_ref[n]) * enter_ref[n] * c
            full_ref[here, :] = out
        return carry

    lax.fori_loop(0, length // SUB, block, 0)
    for g in range(groups):
        cols = pl.ds(g * LANES, LANES)
        mixed_in = x_ref[:, cols].astype(F32)
        read = full_ref[pl.ds(g, length, stride=SUB), :] + skip_ref[:, cols] * mixed_in
        z = z_ref[:, cols].astype(F32)
        gated_ref[:, cols] = (read * (z / (1.0 + jnp.exp(-z)))).astype(BF16)
    place, half = at_ref[0], at_ref[1]
    count = length // 2
    piece = count // line
    for k in range(line):
        for r in range(2):
            source = pl.multiple_of((2 * ((place + k) % line) + (half ^ r)) * piece, piece)
            order_ref[pl.ds(r * count + k * piece, piece), :] = gated_ref[pl.ds(source, piece), :]
    wide = w_ref.shape[1] // parts
    for j in range(parts):
        cols = pl.ds(j * wide, wide)
        out = jnp.dot(order_ref[...], w_ref[:, cols], preferred_element_type=F32).astype(BF16)
        kept_refs[j][...] = out[:count]
        sent_refs[j][...] = out[count:]


def run_out(at, line, parts, y, total, enter, bc, neg, x, z, skip, w):
    length, channels = x.shape
    wide = w.shape[1]
    vmem = pl.BlockSpec(memory_space=pltpu.VMEM)
    return pl.pallas_call(
        functools.partial(out_kernel, channels // LANES, line, parts),
        out_shape=(jax.ShapeDtypeStruct((length // 2, wide // parts), BF16),) * (2 * parts),
        in_specs=[pl.BlockSpec(memory_space=pltpu.SMEM)] + [vmem] * 9,
        out_specs=(vmem,) * (2 * parts),
        scratch_shapes=[
            pltpu.VMEM((length * SUB, LANES), F32),
            pltpu.VMEM((NSTATE * length, LANES), F32),
            pltpu.VMEM((length, channels), BF16),
            pltpu.VMEM((length, channels), BF16),
        ],
        compiler_params=pltpu.CompilerParams(vmem_limit_bytes=16 * MIB),
        cost_estimate=cost(
            2 * length * channels * wide, 2 * channels * wide + 8 * MIB, NSTATE * length * channels
        ),
        name="readout_project",
    )(at, y, total, enter, bc, neg, x, z, skip, w)


def gate_up_kernel(count, *refs):
    pieces, (gate_ref, up_ref, out_ref, rows_ref) = refs[:count], refs[count:]

    @pl.when(pl.program_id(0) == 0)
    def _():
        at = 0
        for piece in pieces:
            rows_ref[pl.ds(at, piece.shape[0]), :] = piece[...]
            at += piece.shape[0]

    gate = jnp.dot(rows_ref[...], gate_ref[...], preferred_element_type=F32)
    up = jnp.dot(rows_ref[...], up_ref[...], preferred_element_type=F32)
    out_ref[...] = (gate / (1.0 + jnp.exp(-gate)) * up).astype(BF16)


def gate_up(pieces, w_gate, w_up):
    depth, hidden = w_gate.shape
    rows = sum(p.shape[0] for p in pieces)
    tile = min(256, hidden)
    weight = pl.BlockSpec((depth, tile), lambda j: (0, j))
    return pl.pallas_call(
        functools.partial(gate_up_kernel, len(pieces)),
        out_shape=jax.ShapeDtypeStruct((rows, hidden), BF16),
        grid=(hidden // tile,),
        in_specs=[pl.BlockSpec(p.shape, lambda j: (0, 0)) for p in pieces] + [weight, weight],
        out_specs=pl.BlockSpec((rows, tile), lambda j: (0, j)),
        scratch_shapes=[pltpu.VMEM((rows, depth), BF16)],
        compiler_params=pltpu.CompilerParams(vmem_limit_bytes=52 * MIB),
        cost_estimate=cost(4 * rows * depth * hidden, 4 * depth * hidden + 2 * rows * depth),
        name="gate_up",
    )(*pieces, w_gate, w_up)


def down_kernel(rows_ref, w_ref, *outs):
    out = jnp.dot(rows_ref[...], w_ref[...], preferred_element_type=F32).astype(BF16)
    start = 0
    for ref in outs:
        ref[...] = out[start : start + ref.shape[0]]
        start += ref.shape[0]


def down(rows, sizes, w_down):
    hidden, wide = w_down.shape
    tile = min(512, wide)
    return pl.pallas_call(
        down_kernel,
        out_shape=tuple(jax.ShapeDtypeStruct((n, wide), BF16) for n in sizes),
        grid=(wide // tile,),
        in_specs=[
            pl.BlockSpec(rows.shape, lambda j: (0, 0)),
            pl.BlockSpec((hidden, tile), lambda j: (0, j)),
        ],
        out_specs=tuple(pl.BlockSpec((n, tile), lambda j: (0, j)) for n in sizes),
        compiler_params=pltpu.CompilerParams(vmem_limit_bytes=52 * MIB),
        cost_estimate=cost(
            2 * rows.shape[0] * hidden * wide, 2 * hidden * wide + 2 * rows.shape[0] * (hidden + wide)
        ),
        name="down",
    )(rows, w_down)


def add_up(*parts):
    return sum(p.astype(F32) for p in parts)


def along_line(block, distance):
    size = lax.axis_size("expert")
    return lax.ppermute(block, "expert", [(e, (e + 2 * distance) % size) for e in range(size)])


def cross(block, turn):
    owners, dps = lax.axis_size("expert"), lax.axis_size("dp")
    route = []
    for e in range(owners):
        for core in range(2):
            for d in range(dps):
                to = (e ^ 1, core, d) if core == turn else (e, core, d ^ 1)
                route.append(((e * 2 + core) * dps + d, (to[0] * 2 + core) * dps + to[2]))
    return lax.ppermute(block, ("expert", "context", "dp"), route)


def after(block, other):
    return lax.optimization_barrier((block, other))[0]


class Chunk:
    def __init__(self, packed, line, square):
        self.line, self.square, self.packed = line, square, packed

    def send(self):
        size = self.packed.shape[0] // self.line
        parts = [self.packed[size * s : size * (s + 1)] for s in range(self.line)]
        self.arrived = [parts[0]] + [along_line(parts[s], s) for s in range(1, self.line)]

    def first(self):
        self.own = jnp.concatenate(self.arrived, axis=0)
        self.near = cross(self.own, 0) if self.square else swap_pair(self.own)

    def second(self):
        self.two = jnp.concatenate([self.own, self.near], axis=0)
        if self.square:
            self.two_far = shift(self.two, "context", 1)
            self.four = cross(self.two, 1)
        else:
            self.four = lax.all_gather(self.two, ("context", "dp"), axis=0, tiled=True)

    def third(self):
        self.pieces, self.sizes = [self.four], (self.four.shape[0],)
        if self.square:
            self.pieces = [self.two, self.four, self.two_far, shift(self.four, "context", 1)]
            self.sizes = (2 * self.two.shape[0],) * 2

    def work_first(self, w_gate, w_up, *others):
        pieces = lax.optimization_barrier((self.pieces, others))[0]
        self.hidden = gate_up(pieces, w_gate, w_up)

    def work_second(self, w_down, *others):
        self.outs = down(lax.optimization_barrier((self.hidden, others))[0], self.sizes, w_down)

    def back_first(self):
        if self.square:
            self.far = shift(self.outs[1], "context", 1)

    def back_second(self):
        rows = self.own.shape[0]
        if self.square:
            both = add_up(self.outs[0], self.far)
            self.kept, self.go = both[: 2 * rows], both[2 * rows :].astype(BF16)
            self.far = cross(self.go, 1)
        else:
            both = lax.psum_scatter(self.outs[0], ("context", "dp"), scatter_dimension=0, tiled=True)
            self.kept, self.go = both, both[rows:]

    def back_third(self):
        rows = self.own.shape[0]
        if self.square:
            two = add_up(self.kept, self.far)
            self.kept, self.go = two[:rows], two[rows:].astype(BF16)
            self.far = cross(self.go, 0)
        else:
            self.kept, self.far = self.kept[:rows], swap_pair(self.go)

    def home(self):
        result = add_up(self.kept, self.far).astype(BF16)
        size = result.shape[0] // self.line
        parts = [result[size * s : size * (s + 1)] for s in range(self.line)]
        self.result = parts[1]
        self.came = [parts[0]] + [along_line(parts[s], -s) for s in range(1, self.line)]


def on_device(
    residual,
    x_raw,
    z_gate,
    conv_w,
    conv_b,
    xproj_w,
    dtproj_w,
    dt_bias,
    a_rate,
    skip_gain,
    out_w,
    norm_gain,
    route_ids,
    route_w,
    w_gate,
    w_up,
    w_down,
):
    owners, contexts, dps = (lax.axis_size(a) for a in ("expert", "context", "dp"))
    me = lax.axis_index("expert")
    place, half = me // 2, me % 2
    line = owners // 2
    length, channels = x_raw.shape[2:]
    width = residual.shape[3]
    row_count = residual.shape[2]

    values = x_raw[0, 0]
    prior_rim = from_behind(values[length - (CONV - 1) :], "context", 1)
    padded = jnp.concatenate([prior_rim, values], axis=0).astype(F32)
    conv_sum = conv_b[None, :] + sum(
        (
            conv_w[lag_index][None, :] * padded[lag_index : lag_index + length]
            for lag_index in range(CONV)
        )
    )
    mixed_in = jax.nn.silu(conv_sum).astype(BF16)
    projected = jnp.dot(mixed_in, xproj_w, preferred_element_type=F32).astype(BF16)
    shares = projected.reshape(line, length // line, -1)

    def share_of(s):
        return lax.dynamic_index_in_dim(shares, (place + s) % line, 0, keepdims=False)

    share = add_up(share_of(0), *[along_line(share_of(s), s) for s in range(1, line)]).astype(BF16)
    share = add_up(share, swap_pair(share)).astype(BF16)
    pieces = [share] + [along_line(share, s) for s in range(1, line)]

    neg = -a_rate.reshape(NSTATE, channels // LANES, LANES)
    neg = jnp.pad(neg, ((0, 0), (0, SUB - channels // LANES), (0, 0)))
    where = jnp.stack([place, half]).astype(jnp.int32)
    y, total, end, bc = run_scan(where, pieces, dtproj_w, dt_bias[None, :], neg, mixed_in)
    enter = from_behind(end, "context", 1)
    for step in range(contexts - 2):
        decay = jnp.exp(total[-SUB:][None] * neg)
        enter = from_behind(end + decay * enter, "context", 1)
    parts = 4
    part = width // parts
    cut = run_out(
        where, line, parts, y, total, enter, bc, neg, mixed_in, z_gate[0, 0], skip_gain[None, :], out_w
    )
    kept, sent = cut[:parts], cut[parts:]
    sums, got = [], []
    for k in range(parts):
        block = sent[k] if k < 2 else after(sent[k], got[k - 2])
        got.append(swap_pair(block))
    for k in range(parts):
        both = add_up(kept[k], got[k]).reshape(line, row_count, part)
        sums.append(
            add_up(both[0], *[along_line(both[s].astype(BF16), s) for s in range(1, line)])
        )
    mixer_out = jnp.concatenate(sums, axis=1)

    stream_f = (residual[0, 0].astype(F32) + mixer_out).astype(BF16).astype(F32)
    normed = (
        stream_f
        * lax.rsqrt(jnp.mean(stream_f * stream_f, axis=1, keepdims=True) + 1e-05)
        * norm_gain[None, :]
    ).astype(BF16)
    ids, weights = route_ids[0, 0], route_w[0, 0]
    capacity = min(row_count, 8 * ((3 * row_count * TOP + 16 * line - 1) // (16 * line)))
    chunks = capacity // 8
    named = jnp.any(ids[:, :, None] == jnp.arange(line, dtype=jnp.int32), axis=1)
    rank = jnp.cumsum(named.astype(jnp.int32), axis=0) - 1
    chosen = ids[:, :, None] == jnp.arange(line, dtype=jnp.int32)
    rank_of = jnp.sum(jnp.where(chosen, rank[:, None, :], 0), axis=2)
    slot_of = (rank_of // 8) * (line * 8) + (ids - place + line) % line * 8 + rank_of % 8
    slots = jnp.arange(line * capacity, dtype=jnp.int32)
    hits = slot_of[:, :, None] == slots
    placing = jnp.any(hits, axis=1).astype(BF16)
    weighting = jnp.sum(jnp.where(hits, weights[:, :, None], 0.0), axis=1)
    square = contexts == 2 and dps == 2
    rows = line * 8
    chunk = []
    for k in range(chunks):
        packed = lax.dot_general(
            placing[:, k * rows : (k + 1) * rows],
            normed,
            (((0,), (0,)), ((), ())),
            preferred_element_type=F32,
        ).astype(BF16)
        chunk.append(Chunk(packed, line, square))
        chunk[k].send()
    for k in range(chunks):
        chunk[k].first()
        chunk[k].second()
        chunk[k].third()
    for k in range(chunks):
        before, between = [], []
        if k + 1 < chunks:
            before.append(chunk[k + 1].two)
            between.append(chunk[k + 1].four)
        if k + 2 < chunks:
            between.append(chunk[k + 2].own)
        if k >= 1:
            between.append(chunk[k - 1].go)
            chunk[k - 1].back_third()
        if k >= 2:
            before.append(chunk[k - 2].result_go)
        chunk[k].work_first(w_gate[0], w_up[0], *before)
        chunk[k].work_second(w_down[0], *between)
        chunk[k].back_first()
        chunk[k].back_second()
        chunk[k].result_go = chunk[k].go
    for k in range(chunks):
        if k == chunks - 1:
            chunk[k].back_third()
        chunk[k].home()
    expert_sum = 0.0
    for k in range(chunks):
        expert_sum = expert_sum + jnp.dot(
            weighting[:, k * rows : (k + 1) * rows],
            jnp.concatenate(chunk[k].came, axis=0).astype(F32),
            precision=lax.Precision.HIGHEST,
            preferred_element_type=F32,
        )
    mixed = (stream_f + expert_sum).astype(BF16)
    return mixed.reshape(1, 1, row_count, width)


def solution(mesh):
    placed = (
        P("dp", "context", "expert", None),
        P("dp", "context", None, "expert"),
        P("dp", "context", None, "expert"),
        P(None, "expert"),
        P("expert"),
        P("expert", None),
        P(None, "expert"),
        P("expert"),
        P(None, "expert"),
        P("expert"),
        P("expert", None),
        P(),
        P("dp", "context", "expert", None),
        P("dp", "context", "expert", None),
        P("expert", None, ("context", "dp")),
        P("expert", None, ("context", "dp")),
        P("expert", ("context", "dp"), None),
    )
    return jax.shard_map(
        on_device,
        mesh=mesh,
        in_specs=placed,
        out_specs=P("dp", "context", "expert", None),
        check_vma=False,
    )
```

time: 265 us -> 271 us (1.023)
  blocking collectives: 33.8 us -> 0 us
  starting transfers between devices: 57.1 us -> 85.7 us
  Pallas kernels: 67.4 us -> 86.2 us
  waiting for transfers between devices: 77.1 us -> 71.1 us
    ppermute x18 -> x48, starting transfers between devices: 33.6 us -> 74.2 us  [the longest x36 57.8 us: along_line(): lax.ppermute(block, 'expert', [(e, (e + 2 * distance) % size) for e in ra...]
    ppermute x18 -> x48, waiting for transfers between devices: 14.5 us -> 51.8 us  [the longest x12 34.8 us: cross(): return lax.ppermute(block, ('expert', 'context', 'dp'), route)]
    all_to_all x2 -> x0, blocking collectives: 33.8 us -> none  [the longest x1 18.9 us: on_device(): lax.all_to_all(packed, 'expert', split_axis=0, concat_axis=0, axis_index_...]
    ppermute x8 -> x5, waiting for transfers between devices: 48.3 us -> 17.8 us  [swap_pair(): return lax.ppermute(block, 'expert', [(i, i ^ 1) for i in range(size)])]
    pallas_call x4 -> x5, Pallas kernels: 28.5 us -> 44.5 us  [the longest x3 29.2 us: down(): pl.pallas_call(down_kernel, out_shape=tuple((jax.ShapeDtypeStruct((n, wid...]
    ppermute x13 -> x9, starting transfers between devices: 9.17 us -> 1.17 us  [shift(): lax.ppermute(block, axis, [(i, (i + distance) % size) for i in range(size)])]
    all_to_all x1 -> x0, waiting for transfers between devices: 7.58 us -> none  [on_device(): lax.all_to_all(jnp.broadcast_to(share[None], (owners,) + share.shape), 'e...]
    ppermute x13 -> x9, waiting for transfers between devices: 6.74 us -> 1.38 us  [shift(): lax.ppermute(block, axis, [(i, (i + distance) % size) for i in range(size)])]
  transfers between devices with their start and end apart: 42 -> 64, of which waited for: 16 -> 27; matrix products, arithmetic and copies ran while one was open for 2% -> 2% of each run, Pallas kernels for 13% -> 26%
where the time goes in v2:
time: 271 us; the launch traced here: 270 us
  Pallas kernels  86.2 us (32%)
  starting transfers between devices  85.7 us (32%)
  waiting for transfers between devices  71.1 us (26%)
  local copies, waits for them, and re-layouts  16.4 us (6%)
  other arithmetic  6.53 us (2%)
  matrix products  3.24 us (1%)
    ppermute x36, starting transfers between devices, along_line(): lax.ppermute(block, 'expert', [(e, (e + 2 * distance) % size) for e in ra...  57.8 us
    pallas_call x3, Pallas kernels, gate_up(): pl.pallas_call(functools.partial(gate_up_kernel, len(pieces)), out_shape=...  41.7 us
    ppermute x12, waiting for transfers between devices, cross(): return lax.ppermute(block, ('expert', 'context', 'dp'), route)  34.8 us
    pallas_call x3, Pallas kernels, down(): pl.pallas_call(down_kernel, out_shape=tuple((jax.ShapeDtypeStruct((n, wid...  29.2 us
    ppermute x5, waiting for transfers between devices, swap_pair(): return lax.ppermute(block, 'expert', [(i, i ^ 1) for i in range(size)])  17.8 us
    ppermute x36, waiting for transfers between devices, along_line(): lax.ppermute(block, 'expert', [(e, (e + 2 * distance) % size) for e in ra...  17.1 us
    ppermute x12, starting transfers between devices, cross(): return lax.ppermute(block, ('expert', 'context', 'dp'), route)  16.4 us
    unnamed x66, local copies, waits for them, and re-layouts  13.9 us
  transfers between devices with their start and end apart: 64, of which 27 were waited for; matrix products, arithmetic and copies ran while one was open for 2% of the time, Pallas kernels for 26%

profile of v2, /device:TPU:0, one launch (start us, length us, event | category | flops | bytes accessed | tf_op | source)
XLA Modules:
  0.0 270.0 jit_solution(15395088957160294409)
XLA Ops:
  0.8 2.3 collective-permute-start
  7.3 2.5 collective-permute-start.1
  9.7 2.6 collective-permute-start.2
  13.9 2.3 collective-permute-done.2
  18.2 2.5 collective-permute-done.4
  21.8 2.6 collective-permute-start.6
  29.5 6.9 %state_scan.1 = (f32[2048,128]{1,0:T(8,128)S(1)}, f32[2048,128]{1,0:T(8,128)S(1)}, f32[16,8,128]{2,1,0:T(8,128)S(1)}, bf16[256,32]{1,0:T(8,128)(2,1)S(1)}) custom-call(s32[2]{0:T(128)S(1)} %pad_add_fusion.place_ref.at_ref, bf16[64,288]{1,0:T(8,128)(2,1)S(1)} %add_convert_fusion.refs_0_, bf16[64,288]{1,0:T(8,128)(2,1)S(1)} %collective-permute-done.5.refs_1_, ...), custom_call_target="tpu_custom_call" | custom-call | flops 200000000 | bytes 4194304 | tf_op jit(solution)/shard_map/state_scan/pallas_call | solution.py:104
  39.3 3.4 %copy-done.2 = bf16[1024,4096]{1,0:T(8,128)(2,1)S(1)} copy-done((bf16[1024,4096]{1,0:T(8,128)(2,1)S(1)}, bf16[1024,4096]{1,0:T(8,128)(2,1)}, u32[]{:S(2)}) %copy-start.2) | copy-done | bytes 8388632
  43.5 8.4 %readout_project.1 = (bf16[128,1024]{1,0:T(8,128)(2,1)S(1)}, bf16[128,1024]{1,0:T(8,128)(2,1)S(1)}, bf16[128,1024]{1,0:T(8,128)(2,1)S(1)}, bf16[128,1024]{1,0:T(...) custom-call(s32[2]{0:T(128)S(1)} %pad_add_fusion.place_ref.at_ref, ...), custom_call_target="tpu_custom_call" | custom-call | flops 2147483648 | bytes 16777216 | tf_op jit(solution)/shard_map/readout_project/pallas_call | solution.py:171
  58.4 7.1 %collective-permute-done.9 = bf16[128,1024]{1,0:T(8,128)(2,1)S(1)} collective-permute-done((bf16[128,1024]{1,0:T(8,128)(2,1)}, bf16[128,1024]{1,0:T(8,128)(2,1)S(1)}, u32[]{:S(2)}, u32[]{:S(2)}) %collective-permute-start.9) | collective-permute-done | bytes 262176 | tf_op jit(solution)/shard_map/ppermute | solution.py:34
  67.2 4.0 %collective-permute-done.13 = bf16[128,1024]{1,0:T(8,128)(2,1)S(1)} collective-permute-done((bf16[128,1024]{1,0:T(8,128)(2,1)}, bf16[128,1024]{1,0:T(8,128)(2,1)S(1)}, u32[]{:S(2)}, u32[]{:S(2)}) %collective-permute-start.13) | collective-permute-done | bytes 262176 | tf_op jit(solution)/shard_map/ppermute | solution.py:34
  72.7 4.1 %collective-permute-done.17 = bf16[128,1024]{1,0:T(8,128)(2,1)S(1)} collective-permute-done((bf16[128,1024]{1,0:T(8,128)(2,1)}, bf16[128,1024]{1,0:T(8,128)(2,1)S(1)}, u32[]{:S(2)}, u32[]{:S(2)}) %collective-permute-start.17) | collective-permute-done | bytes 262176 | tf_op jit(solution)/shard_map/ppermute | solution.py:34
  87.7 2.8 %collective-permute-start.19 = (bf16[32,1024]{1,0:T(8,128)(2,1)S(1)}, bf16[32,1024]{1,0:T(8,128)(2,1)S(1)}, u32[]{:S(2)}, u32[]{:S(2)}) collective-permute-start(bf16[32,1024]{1,0:T(8,128)(2,1)S(1)} %get-tuple-element.120), channel_id=1, source_target_pairs={{0,16},{4,20},{8,24},{12,28},{16,0},{20,4},{24,8},{28,12},{1,17},{... | collective-permute-start | bytes 196616 | tf_op jit(solution)/shard_map/ppermute | solution.py:257
  90.6 4.3 %collective-permute-start.20 = (bf16[32,1024]{1,0:T(8,128)(2,1)S(1)}, bf16[32,1024]{1,0:T(8,128)(2,1)S(1)}, u32[]{:S(2)}, u32[]{:S(2)}) collective-permute-start(bf16[32,1024]{1,0:T(8,128)(2,1)S(1)} %get-tuple-element.119), channel_id=1, source_target_pairs={{0,24},{4,28},{8,0},{12,4},{16,8},{20,12},{24,16},{28,20},{1,25},{... | collective-permute-start | bytes 196616 | tf_op jit(solution)/shard_map/ppermute | solution.py:257
  94.9 2.6 collective-permute-start.23
  110.6 2.6 collective-permute-start.27
  114.1 3.4 %collective-permute-start.38 = (bf16[8,4096]{1,0:T(8,128)(2,1)S(1)}, bf16[8,4096]{1,0:T(8,128)(2,1)S(1)}, u32[]{:S(2)}, u32[]{:S(2)}) collective-permute-start(bf16[8,4096]{1,0:T(8,128)(2,1)S(1)} %get-tuple-element.110), channel_id=1, source_target_pairs={{0,16},{4,20},{8,24},{12,28},{16,0},{20,4},{24,8},{28,12},{1,17},{... | collective-permute-start | bytes 196616 | tf_op jit(solution)/shard_map/ppermute | solution.py:257
  117.6 3.6 %collective-permute-start.39 = (bf16[8,4096]{1,0:T(8,128)(2,1)S(1)}, bf16[8,4096]{1,0:T(8,128)(2,1)S(1)}, u32[]{:S(2)}, u32[]{:S(2)}) collective-permute-start(bf16[8,4096]{1,0:T(8,128)(2,1)S(1)} %get-tuple-element.109), channel_id=1, source_target_pairs={{0,24},{4,28},{8,0},{12,4},{16,8},{20,12},{24,16},{28,20},{1,25},{... | collective-permute-start | bytes 196616 | tf_op jit(solution)/shard_map/ppermute | solution.py:257
  125.0 10.7 %collective-permute-done.28 = bf16[32,4096]{1,0:T(8,128)(2,1)S(1)} collective-permute-done((bf16[32,4096]{1,0:T(8,128)(2,1)S(1)}, bf16[32,4096]{1,0:T(8,128)(2,1)S(1)}, u32[]{:S(2)}, u32[]{:S(2)}) %collective-permute-start.28) | collective-permute-done | bytes 262176 | tf_op jit(solution)/shard_map/ppermute | solution.py:268
  137.4 7.6 %collective-permute-done.29.refs_1_ = bf16[64,4096]{1,0:T(8,128)(2,1)S(1)} collective-permute-done((bf16[64,4096]{1,0:T(8,128)(2,1)S(1)}, bf16[64,4096]{1,0:T(8,128)(2,1)S(1)}, u32[]{:S(2)}, u32[]{:S(2)}) %collective-permute-start.29) | collective-permute-done | bytes 524320 | tf_op jit(solution)/shard_map/ppermute | solution.py:268
  147.7 13.9 %gate_up.3.rows_ref = bf16[256,1536]{1,0:T(8,128)(2,1)} custom-call(bf16[64,4096]{1,0:T(8,128)(2,1)S(1)} %constant_dynamic-update-slice_fusion.refs_0_, bf16[64,4096]{1,0:T(8,128)(2,1)S(1)} %collective-permute-done.29.refs_1_, bf16[64,4096]{1,0:T(8,128)(2,1)S(1)} %collective-permute-done.30.refs_2_, bf16[64,4096]{1,0:T(8,128)(2,1)} %copy-done.21, ...), custom_call_target="tpu_custom_call" | custom-call | flops 6442450944 | bytes 27262976 | tf_op jit(solution)/shard_map/gate_up/pallas_call | solution.py:210
  162.7 9.7 %down.3 = (bf16[128,4096]{1,0:T(8,128)(2,1)S(1)}, bf16[128,4096]{1,0:T(8,128)(2,1)}) custom-call(bf16[256,1536]{1,0:T(8,128)(2,1)S(1)} %copy-done.4, bf16[1536,4096]{1,0:T(8,128)(2,1)} %bitcast.50), custom_call_target="tpu_custom_call" | custom-call | flops 3221225472 | bytes 15466496 | tf_op jit(solution)/shard_map/down/pallas_call | solution.py:234
  175.0 6.9 %collective-permute-done.49.refs_1_ = bf16[64,4096]{1,0:T(8,128)(2,1)S(1)} collective-permute-done((bf16[64,4096]{1,0:T(8,128)(2,1)S(1)}, bf16[64,4096]{1,0:T(8,128)(2,1)S(1)}, u32[]{:S(2)}, u32[]{:S(2)}) %collective-permute-start.49) | collective-permute-done | bytes 524320 | tf_op jit(solution)/shard_map/ppermute | solution.py:268
  184.3 13.9 %gate_up.4.rows_ref = bf16[256,1536]{1,0:T(8,128)(2,1)} custom-call(bf16[64,4096]{1,0:T(8,128)(2,1)S(1)} %constant_dynamic-update-slice_fusion.5.refs_0_, bf16[64,4096]{1,0:T(8,128)(2,1)S(1)} %collective-permute-done.36.refs_1_, bf16[64,4096]{1,0:T(8,128)(2,1)S(1)} %collective-permute-done.46.refs_2_, bf16[64,4096]{1,0:T(8,128)(2,1)} %copy-done.20, ...), custom_call_target="tpu_custom_call" | custom-call | flops 6442450944 | bytes 27262976 | tf_op jit(solution)/shard_map/gate_up/pallas_call | solution.py:210
  199.4 9.7 %down.4 = (bf16[128,4096]{1,0:T(8,128)(2,1)S(1)}, bf16[128,4096]{1,0:T(8,128)(2,1)}) custom-call(bf16[256,1536]{1,0:T(8,128)(2,1)S(1)} %copy-done.5, bf16[1536,4096]{1,0:T(8,128)(2,1)} %bitcast.51), custom_call_target="tpu_custom_call" | custom-call | flops 3221225472 | bytes 15466496 | tf_op jit(solution)/shard_map/down/pallas_call | solution.py:234
  210.9 13.9 %gate_up.5.rows_ref = bf16[256,1536]{1,0:T(8,128)(2,1)} custom-call(bf16[64,4096]{1,0:T(8,128)(2,1)S(1)} %constant_dynamic-update-slice_fusion.10.refs_0_, bf16[64,4096]{1,0:T(8,128)(2,1)S(1)} %collective-permute-done.49.refs_1_, bf16[64,4096]{1,0:T(8,128)(2,1)S(1)} %collective-permute-done.56.refs_2_, bf16[64,4096]{1,0:T(8,128)(2,1)} %copy-done.19, ...), custom_call_target="tpu_custom_call" | custom-call | flops 6442450944 | bytes 27262976 | tf_op jit(solution)/shard_map/gate_up/pallas_call | solution.py:210
  226.0 9.7 %down.5 = (bf16[128,4096]{1,0:T(8,128)(2,1)S(1)}, bf16[128,4096]{1,0:T(8,128)(2,1)}) custom-call(bf16[256,1536]{1,0:T(8,128)(2,1)S(1)} %copy-done.3, bf16[1536,4096]{1,0:T(8,128)(2,1)} %bitcast.52), custom_call_target="tpu_custom_call" | custom-call | flops 3221225472 | bytes 15466496 | tf_op jit(solution)/shard_map/down/pallas_call | solution.py:234
  240.2 3.0 %collective-permute-done.52 = bf16[32,4096]{1,0:T(8,128)(2,1)S(1)} collective-permute-done((bf16[32,4096]{1,0:T(8,128)(2,1)S(1)}, bf16[32,4096]{1,0:T(8,128)(2,1)S(1)}, u32[]{:S(2)}, u32[]{:S(2)}) %collective-permute-start.52) | collective-permute-done | bytes 262176 | tf_op jit(solution)/shard_map/ppermute | solution.py:268
  243.3 4.9 %collective-permute-done.59 = bf16[64,4096]{1,0:T(8,128)(2,1)S(1)} collective-permute-done((bf16[64,4096]{1,0:T(8,128)(2,1)S(1)}, bf16[64,4096]{1,0:T(8,128)(2,1)S(1)}, u32[]{:S(2)}, u32[]{:S(2)}) %collective-permute-start.59) | collective-permute-done | bytes 524320 | tf_op jit(solution)/shard_map/ppermute | solution.py:268
  249.9 3.3 %collective-permute-start.53 = (bf16[8,4096]{1,0:T(8,128)(2,1)S(1)}, bf16[8,4096]{1,0:T(8,128)(2,1)S(1)}, u32[]{:S(2)}, u32[]{:S(2)}) collective-permute-start(bf16[8,4096]{1,0:T(8,128)(2,1)S(1)} %get-tuple-element.92), channel_id=1, source_target_pairs={{0,24},{4,28},{8,0},{12,4},{16,8},{20,12},{24,16},{28,20},{1,25},{... | collective-permute-start | bytes 196616 | tf_op jit(solution)/shard_map/ppermute | solution.py:257
  256.0 3.9 %collective-permute-start.61 = (bf16[8,4096]{1,0:T(8,128)(2,1)S(1)}, bf16[8,4096]{1,0:T(8,128)(2,1)S(1)}, u32[]{:S(2)}, u32[]{:S(2)}) collective-permute-start(bf16[8,4096]{1,0:T(8,128)(2,1)S(1)} %get-tuple-element.96), channel_id=1, source_target_pairs={{0,24},{4,28},{8,0},{12,4},{16,8},{20,12},{24,16},{28,20},{1,25},{... | collective-permute-start | bytes 196616 | tf_op jit(solution)/shard_map/ppermute | solution.py:257
  263.9 2.3 collective-permute-done.62
  (236 shorter events, 87.6 us)
Async XLA Ops:
  56.2 9.3 %collective-permute-start.9 = (bf16[128,1024]{1,0:T(8,128)(2,1)}, bf16[128,1024]{1,0:T(8,128)(2,1)S(1)}, u32[]{:S(2)}, u32[]{:S(2)}) collective-permute-start(bf16[128,1024]{1,0:T(8,128)(2,1)} %get-tuple-element.45), channel_id=1, source_target_pairs={{0,4},{4,0},{8,12},{12,8},{16,20},{20,16},{24,28},{28,24},{1,5},{5... | collective-permute-start | bytes 786440 | tf_op jit(solution)/shard_map/ppermute | solution.py:34
  57.8 13.3 %collective-permute-start.13 = (bf16[128,1024]{1,0:T(8,128)(2,1)}, bf16[128,1024]{1,0:T(8,128)(2,1)S(1)}, u32[]{:S(2)}, u32[]{:S(2)}) collective-permute-start(bf16[128,1024]{1,0:T(8,128)(2,1)} %copy-done.17), channel_id=1, source_target_pairs={{0,4},{4,0},{8,12},{12,8},{16,20},{20,16},{24,28},{28,24},{1,5},{5... | collective-permute-start | bytes 786440 | tf_op jit(solution)/shard_map/ppermute | solution.py:34
  65.5 11.2 %collective-permute-start.17 = (bf16[128,1024]{1,0:T(8,128)(2,1)}, bf16[128,1024]{1,0:T(8,128)(2,1)S(1)}, u32[]{:S(2)}, u32[]{:S(2)}) collective-permute-start(bf16[128,1024]{1,0:T(8,128)(2,1)} %copy-done.16), channel_id=1, source_target_pairs={{0,4},{4,0},{8,12},{12,8},{16,20},{20,16},{24,28},{28,24},{1,5},{5... | collective-permute-start | bytes 786440 | tf_op jit(solution)/shard_map/ppermute | solution.py:34
  71.1 10.8 %collective-permute-start.21 = (bf16[128,1024]{1,0:T(8,128)(2,1)}, bf16[128,1024]{1,0:T(8,128)(2,1)S(1)}, u32[]{:S(2)}, u32[]{:S(2)}) collective-permute-start(bf16[128,1024]{1,0:T(8,128)(2,1)} %copy-done.15), channel_id=1, source_target_pairs={{0,4},{4,0},{8,12},{12,8},{16,20},{20,16},{24,28},{28,24},{1,5},{5... | collective-permute-start | bytes 786440 | tf_op jit(solution)/shard_map/ppermute | solution.py:34
  79.0 8.8 %collective-permute-start.11 = (bf16[32,1024]{1,0:T(8,128)(2,1)S(1)}, bf16[32,1024]{1,0:T(8,128)(2,1)S(1)}, u32[]{:S(2)}, u32[]{:S(2)}) collective-permute-start(bf16[32,1024]{1,0:T(8,128)(2,1)S(1)} %get-tuple-element.114), channel_id=1, source_target_pairs={{0,16},{4,20},{8,24},{12,28},{16,0},{20,4},{24,8},{28,12},{1,17},{... | collective-permute-start | bytes 196616 | tf_op jit(solution)/shard_map/ppermute | solution.py:257
  83.4 11.5 %collective-permute-start.15 = (bf16[32,1024]{1,0:T(8,128)(2,1)S(1)}, bf16[32,1024]{1,0:T(8,128)(2,1)S(1)}, u32[]{:S(2)}, u32[]{:S(2)}) collective-permute-start(bf16[32,1024]{1,0:T(8,128)(2,1)S(1)} %get-tuple-element.117), channel_id=1, source_target_pairs={{0,16},{4,20},{8,24},{12,28},{16,0},{20,4},{24,8},{28,12},{1,17},{... | collective-permute-start | bytes 196616 | tf_op jit(solution)/shard_map/ppermute | solution.py:257
  85.2 9.7 %collective-permute-start.16 = (bf16[32,1024]{1,0:T(8,128)(2,1)S(1)}, bf16[32,1024]{1,0:T(8,128)(2,1)S(1)}, u32[]{:S(2)}, u32[]{:S(2)}) collective-permute-start(bf16[32,1024]{1,0:T(8,128)(2,1)S(1)} %get-tuple-element.116), channel_id=1, source_target_pairs={{0,24},{4,28},{8,0},{12,4},{16,8},{20,12},{24,16},{28,20},{1,25},{... | collective-permute-start | bytes 196616 | tf_op jit(solution)/shard_map/ppermute | solution.py:257
  87.7 9.9 %collective-permute-start.18 = (bf16[32,1024]{1,0:T(8,128)(2,1)S(1)}, bf16[32,1024]{1,0:T(8,128)(2,1)S(1)}, u32[]{:S(2)}, u32[]{:S(2)}) collective-permute-start(bf16[32,1024]{1,0:T(8,128)(2,1)S(1)} %get-tuple-element.118), channel_id=1, source_target_pairs={{0,8},{4,12},{8,16},{12,20},{16,24},{20,28},{24,0},{28,4},{1,9},{5... | collective-permute-start | bytes 196616 | tf_op jit(solution)/shard_map/ppermute | solution.py:257
  87.7 11.4 %collective-permute-start.19 = (bf16[32,1024]{1,0:T(8,128)(2,1)S(1)}, bf16[32,1024]{1,0:T(8,128)(2,1)S(1)}, u32[]{:S(2)}, u32[]{:S(2)}) collective-permute-start(bf16[32,1024]{1,0:T(8,128)(2,1)S(1)} %get-tuple-element.120), channel_id=1, source_target_pairs={{0,16},{4,20},{8,24},{12,28},{16,0},{20,4},{24,8},{28,12},{1,17},{... | collective-permute-start | bytes 196616 | tf_op jit(solution)/shard_map/ppermute | solution.py:257
  105.5 8.6 %collective-permute-start.33 = (bf16[8,4096]{1,0:T(8,128)(2,1)S(1)}, bf16[8,4096]{1,0:T(8,128)(2,1)S(1)}, u32[]{:S(2)}, u32[]{:S(2)}) collective-permute-start(bf16[8,4096]{1,0:T(8,128)(2,1)S(1)} %get-tuple-element.100), channel_id=1, source_target_pairs={{0,16},{4,20},{8,24},{12,28},{16,0},{20,4},{24,8},{28,12},{1,17},{... | collective-permute-start | bytes 196616 | tf_op jit(solution)/shard_map/ppermute | solution.py:257
  108.1 9.5 %collective-permute-start.25 = (bf16[8,4096]{1,0:T(8,128)(2,1)S(1)}, bf16[8,4096]{1,0:T(8,128)(2,1)S(1)}, u32[]{:S(2)}, u32[]{:S(2)}) collective-permute-start(bf16[8,4096]{1,0:T(8,128)(2,1)S(1)} %get-tuple-element.106), channel_id=1, source_target_pairs={{0,8},{4,12},{8,16},{12,20},{16,24},{20,28},{24,0},{28,4},{1,9},{5... | collective-permute-start | bytes 196616 | tf_op jit(solution)/shard_map/ppermute | solution.py:257
  109.2 12.0 %collective-permute-start.26 = (bf16[8,4096]{1,0:T(8,128)(2,1)S(1)}, bf16[8,4096]{1,0:T(8,128)(2,1)S(1)}, u32[]{:S(2)}, u32[]{:S(2)}) collective-permute-start(bf16[8,4096]{1,0:T(8,128)(2,1)S(1)} %get-tuple-element.105), channel_id=1, source_target_pairs={{0,16},{4,20},{8,24},{12,28},{16,0},{20,4},{24,8},{28,12},{1,17},{... | collective-permute-start | bytes 196616 | tf_op jit(solution)/shard_map/ppermute | solution.py:257
  110.6 12.2 %collective-permute-start.27 = (bf16[8,4096]{1,0:T(8,128)(2,1)S(1)}, bf16[8,4096]{1,0:T(8,128)(2,1)S(1)}, u32[]{:S(2)}, u32[]{:S(2)}) collective-permute-start(bf16[8,4096]{1,0:T(8,128)(2,1)S(1)} %get-tuple-element.104), channel_id=1, source_target_pairs={{0,24},{4,28},{8,0},{12,4},{16,8},{20,12},{24,16},{28,20},{1,25},{... | collective-permute-start | bytes 196616 | tf_op jit(solution)/shard_map/ppermute | solution.py:257
  114.1 9.2 %collective-permute-start.37 = (bf16[8,4096]{1,0:T(8,128)(2,1)S(1)}, bf16[8,4096]{1,0:T(8,128)(2,1)S(1)}, u32[]{:S(2)}, u32[]{:S(2)}) collective-permute-start(bf16[8,4096]{1,0:T(8,128)(2,1)S(1)} %get-tuple-element.111), channel_id=1, source_target_pairs={{0,8},{4,12},{8,16},{12,20},{16,24},{20,28},{24,0},{28,4},{1,9},{5... | collective-permute-start | bytes 196616 | tf_op jit(solution)/shard_map/ppermute | solution.py:257
  114.1 9.2 %collective-permute-start.38 = (bf16[8,4096]{1,0:T(8,128)(2,1)S(1)}, bf16[8,4096]{1,0:T(8,128)(2,1)S(1)}, u32[]{:S(2)}, u32[]{:S(2)}) collective-permute-start(bf16[8,4096]{1,0:T(8,128)(2,1)S(1)} %get-tuple-element.110), channel_id=1, source_target_pairs={{0,16},{4,20},{8,24},{12,28},{16,0},{20,4},{24,8},{28,12},{1,17},{... | collective-permute-start | bytes 196616 | tf_op jit(solution)/shard_map/ppermute | solution.py:257
  121.2 23.8 %collective-permute-start.35 = (bf16[32,4096]{1,0:T(8,128)(2,1)S(1)}, bf16[32,4096]{1,0:T(8,128)(2,1)S(1)}, u32[]{:S(2)}, u32[]{:S(2)}) collective-permute-start(bf16[32,4096]{1,0:T(8,128)(2,1)S(1)} %pad_maximum_fusion.1), channel_id=1, source_target_pairs={{0,4},{1,5},{2,3},{3,2},{4,0},{5,1},{6,7},{7,6},{8,12},{9,13},{10,... | collective-permute-start | bytes 786440 | tf_op jit(solution)/shard_map/ppermute | solution.py:268
  122.8 12.9 %collective-permute-start.28 = (bf16[32,4096]{1,0:T(8,128)(2,1)S(1)}, bf16[32,4096]{1,0:T(8,128)(2,1)S(1)}, u32[]{:S(2)}, u32[]{:S(2)}) collective-permute-start(bf16[32,4096]{1,0:T(8,128)(2,1)S(1)} %pad_maximum_fusion), channel_id=1, source_target_pairs={{0,4},{1,5},{2,3},{3,2},{4,0},{5,1},{6,7},{7,6},{8,12},{9,13},{10,... | collective-permute-start | bytes 786440 | tf_op jit(solution)/shard_map/ppermute | solution.py:268
  123.4 49.2 %collective-permute-start.48 = (bf16[32,4096]{1,0:T(8,128)(2,1)S(1)}, bf16[32,4096]{1,0:T(8,128)(2,1)S(1)}, u32[]{:S(2)}, u32[]{:S(2)}) collective-permute-start(bf16[32,4096]{1,0:T(8,128)(2,1)S(1)} %pad_maximum_fusion.2), channel_id=1, source_target_pairs={{0,4},{1,5},{2,3},{3,2},{4,0},{5,1},{6,7},{7,6},{8,12},{9,13},{10,... | collective-permute-start | bytes 786440 | tf_op jit(solution)/shard_map/ppermute | solution.py:268
  135.7 9.2 %collective-permute-start.29 = (bf16[64,4096]{1,0:T(8,128)(2,1)S(1)}, bf16[64,4096]{1,0:T(8,128)(2,1)S(1)}, u32[]{:S(2)}, u32[]{:S(2)}) collective-permute-start(bf16[64,4096]{1,0:T(8,128)(2,1)S(1)} %constant_dynamic-update-slice_fusion.refs_0_), channel_id=1, source_target_pairs={{0,1},{1,0},{2,6},{3,7},{4,5},{5,4},{6,2},{7,3},{8,9},{9,8},{10,14... | collective-permute-start | bytes 1572872 | tf_op jit(solution)/shard_map/ppermute | solution.py:268
  137.3 9.3 %collective-permute-start.30 = (bf16[64,4096]{1,0:T(8,128)(2,1)S(1)}, bf16[64,4096]{1,0:T(8,128)(2,1)S(1)}, u32[]{:S(2)}, u32[]{:S(2)}) collective-permute-start(bf16[64,4096]{1,0:T(8,128)(2,1)S(1)} %constant_dynamic-update-slice_fusion.refs_0_), channel_id=1, source_target_pairs={{0,2},{2,0},{1,3},{3,1},{4,6},{6,4},{5,7},{7,5},{8,10},{10,8},{9,1... | collective-permute-start | bytes 1572872 | tf_op jit(solution)/shard_map/ppermute | solution.py:29
  145.0 16.6 %collective-permute-start.36 = (bf16[64,4096]{1,0:T(8,128)(2,1)S(1)}, bf16[64,4096]{1,0:T(8,128)(2,1)S(1)}, u32[]{:S(2)}, u32[]{:S(2)}) collective-permute-start(bf16[64,4096]{1,0:T(8,128)(2,1)S(1)} %constant_dynamic-update-slice_fusion.5.refs_0_), channel_id=1, source_target_pairs={{0,1},{1,0},{2,6},{3,7},{4,5},{5,4},{6,2},{7,3},{8,9},{9,8},{10,14... | collective-permute-start | bytes 1572872 | tf_op jit(solution)/shard_map/ppermute | solution.py:268
  172.5 9.4 %collective-permute-start.40 = (bf16[128,4096]{1,0:T(8,128)(2,1)}, bf16[128,4096]{1,0:T(8,128)(2,1)S(1)}, u32[]{:S(2)}, u32[]{:S(2)}) collective-permute-start(bf16[128,4096]{1,0:T(8,128)(2,1)} %get-tuple-element.60), channel_id=1, source_target_pairs={{0,2},{2,0},{1,3},{3,1},{4,6},{6,4},{5,7},{7,5},{8,10},{10,8},{9,1... | collective-permute-start | bytes 3145736 | tf_op jit(solution)/shard_map/ppermute | solution.py:29
  172.7 9.2 %collective-permute-start.49 = (bf16[64,4096]{1,0:T(8,128)(2,1)S(1)}, bf16[64,4096]{1,0:T(8,128)(2,1)S(1)}, u32[]{:S(2)}, u32[]{:S(2)}) collective-permute-start(bf16[64,4096]{1,0:T(8,128)(2,1)S(1)} %constant_dynamic-update-slice_fusion.10.refs_0_), channel_id=1, source_target_pairs={{0,1},{1,0},{2,6},{3,7},{4,5},{5,4},{6,2},{7,3},{8,9},{9,8},{10,14... | collective-permute-start | bytes 1572872 | tf_op jit(solution)/shard_map/ppermute | solution.py:268
  174.8 34.6 %collective-permute-start.56 = (bf16[64,4096]{1,0:T(8,128)(2,1)S(1)}, bf16[64,4096]{1,0:T(8,128)(2,1)S(1)}, u32[]{:S(2)}, u32[]{:S(2)}) collective-permute-start(bf16[64,4096]{1,0:T(8,128)(2,1)S(1)} %constant_dynamic-update-slice_fusion.10.refs_0_), channel_id=1, source_target_pairs={{0,2},{2,0},{1,3},{3,1},{4,6},{6,4},{5,7},{7,5},{8,10},{10,8},{9,1... | collective-permute-start | bytes 1572872 | tf_op jit(solution)/shard_map/ppermute | solution.py:29
  181.9 27.5 %collective-permute-start.57 = (bf16[64,4096]{1,0:T(8,128)(2,1)S(1)}, bf16[64,4096]{1,0:T(8,128)(2,1)S(1)}, u32[]{:S(2)}, u32[]{:S(2)}) collective-permute-start(bf16[64,4096]{1,0:T(8,128)(2,1)S(1)} %collective-permute-done.49.refs_1_), channel_id=1, source_target_pairs={{0,2},{2,0},{1,3},{3,1},{4,6},{6,4},{5,7},{7,5},{8,10},{10,8},{9,1... | collective-permute-start | bytes 1572872 | tf_op jit(solution)/shard_map/ppermute | solution.py:29
  182.8 26.6 %collective-permute-start.41 = (bf16[64,4096]{1,0:T(8,128)(2,1)S(1)}, bf16[64,4096]{1,0:T(8,128)(2,1)S(1)}, u32[]{:S(2)}, u32[]{:S(2)}) collective-permute-start(bf16[64,4096]{1,0:T(8,128)(2,1)S(1)} %slice.450), channel_id=1, source_target_pairs={{0,1},{1,0},{2,6},{3,7},{4,5},{5,4},{6,2},{7,3},{8,9},{9,8},{10,14... | collective-permute-start | bytes 1572872 | tf_op jit(solution)/shard_map/ppermute | solution.py:268
  209.1 15.7 %collective-permute-start.50 = (bf16[128,4096]{1,0:T(8,128)(2,1)}, bf16[128,4096]{1,0:T(8,128)(2,1)S(1)}, u32[]{:S(2)}, u32[]{:S(2)}) collective-permute-start(bf16[128,4096]{1,0:T(8,128)(2,1)} %get-tuple-element.67), channel_id=1, source_target_pairs={{0,2},{2,0},{1,3},{3,1},{4,6},{6,4},{5,7},{7,5},{8,10},{10,8},{9,1... | collective-permute-start | bytes 3145736 | tf_op jit(solution)/shard_map/ppermute | solution.py:29
  209.5 15.2 %collective-permute-start.42 = (bf16[32,4096]{1,0:T(8,128)(2,1)S(1)}, bf16[32,4096]{1,0:T(8,128)(2,1)S(1)}, u32[]{:S(2)}, u32[]{:S(2)}) collective-permute-start(bf16[32,4096]{1,0:T(8,128)(2,1)S(1)} %slice.453), channel_id=1, source_target_pairs={{0,4},{1,5},{2,3},{3,2},{4,0},{5,1},{6,7},{7,6},{8,12},{9,13},{10,... | collective-permute-start | bytes 786440 | tf_op jit(solution)/shard_map/ppermute | solution.py:268
  225.2 10.8 %collective-permute-start.51 = (bf16[64,4096]{1,0:T(8,128)(2,1)S(1)}, bf16[64,4096]{1,0:T(8,128)(2,1)S(1)}, u32[]{:S(2)}, u32[]{:S(2)}) collective-permute-start(bf16[64,4096]{1,0:T(8,128)(2,1)S(1)} %slice.449), channel_id=1, source_target_pairs={{0,1},{1,0},{2,6},{3,7},{4,5},{5,4},{6,2},{7,3},{8,9},{9,8},{10,14... | collective-permute-start | bytes 1572872 | tf_op jit(solution)/shard_map/ppermute | solution.py:268
  235.8 31.9 %collective-permute-start.43 = (bf16[8,4096]{1,0:T(8,128)(2,1)S(1)}, bf16[8,4096]{1,0:T(8,128)(2,1)S(1)}, u32[]{:S(2)}, u32[]{:S(2)}) collective-permute-start(bf16[8,4096]{1,0:T(8,128)(2,1)S(1)} %get-tuple-element.88), channel_id=1, source_target_pairs={{0,24},{4,28},{8,0},{12,4},{16,8},{20,12},{24,16},{28,20},{1,25},{... | collective-permute-start | bytes 196616 | tf_op jit(solution)/shard_map/ppermute | solution.py:257
  235.9 31.9 %collective-permute-start.44 = (bf16[8,4096]{1,0:T(8,128)(2,1)S(1)}, bf16[8,4096]{1,0:T(8,128)(2,1)S(1)}, u32[]{:S(2)}, u32[]{:S(2)}) collective-permute-start(bf16[8,4096]{1,0:T(8,128)(2,1)S(1)} %get-tuple-element.87), channel_id=1, source_target_pairs={{0,16},{4,20},{8,24},{12,28},{16,0},{20,4},{24,8},{28,12},{1,17},{... | collective-permute-start | bytes 196616 | tf_op jit(solution)/shard_map/ppermute | solution.py:257
  239.0 9.2 %collective-permute-start.59 = (bf16[64,4096]{1,0:T(8,128)(2,1)S(1)}, bf16[64,4096]{1,0:T(8,128)(2,1)S(1)}, u32[]{:S(2)}, u32[]{:S(2)}) collective-permute-start(bf16[64,4096]{1,0:T(8,128)(2,1)S(1)} %slice.448), channel_id=1, source_target_pairs={{0,1},{1,0},{2,6},{3,7},{4,5},{5,4},{6,2},{7,3},{8,9},{9,8},{10,14... | collective-permute-start | bytes 1572872 | tf_op jit(solution)/shard_map/ppermute | solution.py:268
  (60 other events, 383.1 us)
